TPU v7x, 256 devices: a whole 4x4x8 slice. The times are simulated.
256 devices in a mesh: gx: 4 (over y), gy: 16 (over z_lo, x, core), gz: 4 (over z_hi).
Axes of the slice: x: 4, y: 4, z: 8 (z_hi: 4, z_lo: 2; z = z_hi * 2 + z_lo), core: 2. Of those that a mesh axis runs over, the one named last changes fastest.
Arguments:
- species: int32 [4, 16, 4, 128], P('gx', 'gy', 'gz'), may hold values from 0 to 4
- atom_count: int32 [4, 16, 4], P('gx', 'gy', 'gz'), may hold values from 64 to 128, as said below
- send_list: int32 [4, 16, 4, 32], P('gx', 'gy', 'gz'), may hold values from 0 to 127, as said below
- edge_count: int32 [4, 16, 4], P('gx', 'gy', 'gz'), may hold values from 512 to 2560, as said below
- edge_center: int32 [4, 16, 4, 2560], P('gx', 'gy', 'gz'), may hold values from 0 to 127, as said below
- edge_neighbour: int32 [4, 16, 4, 2560], P('gx', 'gy', 'gz'), may hold values from 0 to 991, as said below
- edge_vectors: float32 [4, 16, 4, 3, 2560], P('gx', 'gy', 'gz'), may hold values from -4.6 to 4.6, as said below
- embed: float32 [5, 128], replicated, may hold values from -6 to 6
- w_src: bfloat16 [2, 128, 192], replicated, may hold values from -0.5 to 0.5
- w_rad0: bfloat16 [2, 8, 64], replicated, may hold values from -2 to 2
- w_rad1: bfloat16 [2, 64, 256], replicated, may hold values from -0.75 to 0.75
- w_inv: bfloat16 [2, 64, 128], replicated, may hold values from -0.75 to 0.75
- w_out: bfloat16 [2, 128, 128], replicated, may hold values from -0.5 to 0.5
- w_gate: bfloat16 [2, 128, 64], replicated, may hold values from -0.5 to 0.5
- w_energy: float32 [128], replicated, may hold values from -0.5 to 0.5
Outputs:
- energies: float32 [4, 16, 4, 128], P('gx', 'gy', 'gz')
- forces: float32 [4, 16, 4, 3, 128], P('gx', 'gy', 'gz')
Inputs may be any that keep to these rules, and one draw needn't show every extreme that they name: `atom_count`: domains of dense protein hold more live atoms; some domain is full. `edge_count`: dense domains hold more live edges than watery ones; some domain is full. `send_list`: every entry is a live atom of the domain. `edge_center`: live edges receive at live atoms; edges from the edge_count-th on are 0. `edge_neighbour`: A live edge sends from a live local atom or from a ghost row of another domain inside the slab (never the domain itself); edges from the edge_count-th on are 0. `edge_vectors`: every edge is between 0.9 and 4.6 long.
All inputs are finite; a program needn't handle non-finite values.
Results may differ from a plain program's by a relative error of at most 0.023.
Values may be sent and summed in bfloat16 or wider, within the bound.
A program may use at most 64 MiB of HBM per device.

v0:
```python
import functools
import math

import jax
import jax.numpy as jnp
from jax import lax
from jax.experimental import pallas as pl
from jax.experimental.pallas import tpu as pltpu
from jax.sharding import PartitionSpec as P

RADIAL = 8
CUTOFF = 5.0
TILE = 256
MESH = pl.DeviceIdType.MESH
BF16 = jnp.bfloat16
F32 = jnp.float32


def mm(left, right):
    return lax.dot_general(left, right, (((1,), (0,)), ((), ())), preferred_element_type=F32)


def mm_nt(left, right):
    return lax.dot_general(left, right, (((1,), (1,)), ((), ())), preferred_element_type=F32)


def eye(rows, cols):
    first = lax.broadcasted_iota(jnp.int32, (rows, cols), 0)
    second = lax.broadcasted_iota(jnp.int32, (rows, cols), 1)
    return jnp.where(first == second, 1.0, 0.0).astype(BF16)


def turned(array):
    return mm_nt(eye(array.shape[1], array.shape[1]), array).astype(BF16)


def split(array):
    high = array.astype(BF16).astype(F32)
    return jnp.concatenate([high, array - high], axis=0).astype(BF16)


def joined(array):
    half = array.shape[0] // 2
    return array[:half] + array[half:]


def sum_rows(array):
    return jnp.sum(array, axis=0, keepdims=True)


def sin_cos(angle):
    y = angle - (math.pi / 2)
    y2 = y * y
    sin_y = jnp.full_like(y, -1.0 / math.factorial(11))
    for power in (9, 7, 5, 3, 1):
        sin_y = sin_y * y2 + ((-1.0) ** (power // 2)) / math.factorial(power)
    cos_y = jnp.full_like(y, 1.0 / math.factorial(12))
    for power in (10, 8, 6, 4, 2, 0):
        cos_y = cos_y * y2 + ((-1.0) ** (power // 2)) / math.factorial(power)
    return cos_y, -(sin_y * y)


def body(
    atom_count, edge_count, species, send_list, center, neighbour, vectors,
    embed, w_src, w_rad0, w_rad1, w_inv, w_out, w_gate, w_energy,
    energies, forces,
    onehot, onehot_c, kinds, halo, table, picked, dmsg,
    geo, harm, dbas, basis, slope, rad1, rad2, proj1, lead, agg, agg2, grad_y, grad_d, pull,
    back_send_y, back_recv_y, back_send_x, back_recv_x, back_send_z, back_recv_z,
    f_send_y, f_recv_y, f_send_x, f_recv_x, f_send_z, f_recv_z,
    send_sems, recv_sems,
):
    atoms = species.shape[1]
    edges = center.shape[1]
    sends = send_list.shape[1]
    width = w_out.shape[1]
    chan = w_gate.shape[2]
    rows_x = 3 * sends
    rows_y = 9 * sends
    ghosts = 27 * sends
    tiles = edges // TILE
    own_row = (9 + 3 + 1) * sends

    def step(axis, by):
        size = lax.axis_size(axis)
        return {axis: lax.rem(lax.axis_index(axis) + size + by, size)}

    barrier = pltpu.get_barrier_semaphore()
    for axis in ("gx", "gy", "gz"):
        for by in (1, -1):
            pl.semaphore_signal(barrier, inc=1, device_id=step(axis, by), device_id_type=MESH)

    next_sem = [0]
    started = []

    def send(source, target, axis, by):
        slot = next_sem[0]
        next_sem[0] = slot + 1
        copy = pltpu.make_async_remote_copy(
            src_ref=source, dst_ref=target, send_sem=send_sems.at[slot], recv_sem=recv_sems.at[slot],
            device_id=step(axis, by), device_id_type=MESH,
        )
        copy.start()
        started.append(copy)
        return copy

    def spread_start(ref):
        low = (9 + 3) * sends
        own = ref.at[pl.ds(own_row, sends)]
        return [
            send(own, ref.at[pl.ds(low, sends)], "gz", 1),
            send(own, ref.at[pl.ds(low + 2 * sends, sends)], "gz", -1),
        ]

    def spread_finish(ref, first):
        for copy in first:
            copy.wait_recv()
        middle = ref.at[pl.ds(rows_y + rows_x, rows_x)]
        along_x = [
            send(middle, ref.at[pl.ds(rows_y, rows_x)], "gx", 1),
            send(middle, ref.at[pl.ds(rows_y + 2 * rows_x, rows_x)], "gx", -1),
        ]
        last = []
        for part in (1, 0, 2):
            if part != 1:
                along_x[part // 2].wait_recv()
            rows = ref.at[pl.ds(rows_y + part * rows_x, rows_x)]
            last.append(send(rows, ref.at[pl.ds(part * rows_x, rows_x)], "gy", 1))
            last.append(send(rows, ref.at[pl.ds(2 * rows_y + part * rows_x, rows_x)], "gy", -1))
        for copy in last:
            copy.wait_recv()

    lane = lax.broadcasted_iota(jnp.int32, (atoms, atoms), 0)
    kind_t = jnp.where(lane == species[...], 1.0, 0.0).astype(BF16)
    lend_t = jnp.where(
        lax.broadcasted_iota(jnp.int32, (atoms, sends), 0) == send_list[...], 1.0, 0.0
    ).astype(BF16)
    lend = mm_nt(eye(sends, sends), lend_t).astype(BF16)
    kinds[pl.ds(own_row, sends), :] = mm_nt(lend, kind_t).astype(BF16)
    pl.semaphore_wait(barrier, 6)
    kinds_first = spread_start(kinds)

    live = lax.broadcasted_iota(jnp.int32, (1, edges), 1) < edge_count[0, 0]
    x = jnp.where(live, vectors[0:1, :], 1.0)
    y = jnp.where(live, vectors[1:2, :], 1.0)
    z = jnp.where(live, vectors[2:3, :], 1.0)
    square = x * x + y * y + z * z
    inverse = lax.rsqrt(square)
    distance = square * inverse
    ux, uy, uz = x * inverse, y * inverse, z * inverse
    root = math.sqrt(3.0)
    for row, value in enumerate((ux, uy, uz, inverse)):
        geo[pl.ds(row, 1), :] = value
    for row, value in enumerate((
        ux, uy, uz, root * ux * uy, root * uy * uz, 0.5 * (3.0 * uz * uz - 1.0), root * ux * uz,
        0.5 * root * (ux * ux - uy * uy),
    )):
        harm[pl.ds(row, 1), :] = value
    sine, cosine = sin_cos(distance * (math.pi / CUTOFF))
    ratio = distance * (1.0 / CUTOFF)
    rest = 1.0 - ratio * ratio
    scale = rest * rest * inverse
    dscale = -(4.0 / CUTOFF) * rest * ratio * inverse - scale * inverse
    sin_k, cos_k = sine, cosine
    basis[...] = jnp.zeros_like(basis)
    for k in range(1, RADIAL + 1):
        basis[pl.ds(k - 1, 1), :] = sin_k * scale
        dbas[pl.ds(k - 1, 1), :] = (k * math.pi / CUTOFF) * cos_k * scale + sin_k * dscale
        sin_k, cos_k = sin_k * cosine + cos_k * sine, cos_k * cosine - sin_k * sine

    near = neighbour[...]
    ghost = near - atoms
    part_a = jnp.where(ghost >= rows_y, 1, 0) + jnp.where(ghost >= 2 * rows_y, 1, 0)
    ghost = ghost - rows_y * part_a
    part_b = jnp.where(ghost >= rows_x, 1, 0) + jnp.where(ghost >= 2 * rows_x, 1, 0)
    ghost = ghost - rows_x * part_b + rows_x * part_a + rows_y * part_b + atoms
    place = jnp.where(live, jnp.where(near < atoms, near, ghost), -1)
    middle_atom = jnp.where(live, center[...], -1)
    lead[pl.ds(0, 1), :] = place
    lead[pl.ds(1, 1), :] = middle_atom

    src1_t = turned(w_src[0])
    src2_t = turned(w_src[1])
    rad0_t = jnp.concatenate(
        [
            turned(jnp.concatenate([w_rad0[l].astype(F32), jnp.zeros((8, w_rad0.shape[2]), F32)], axis=0).astype(BF16))
            .astype(F32)
            for l in range(2)
        ],
        axis=0,
    ).astype(BF16)
    hid = w_rad0.shape[2]
    rad1_t1 = turned(w_rad1[0][:, : width + chan])
    rad1_t2 = turned(w_rad1[1][:, :width])
    inv_t = turned(w_inv[1])
    out1_t = turned(w_out[0])
    out2_t = turned(w_out[1])
    gate_t = turned(w_gate[0])
    embed_rows = jnp.concatenate([embed[...], jnp.zeros((16 - embed.shape[0], width), F32)], axis=0)
    embed_t = turned(embed_rows.astype(BF16))
    kind_proj = mm(src1_t, embed_t).astype(BF16)
    start = mm(embed_t, kind_t[:16, :])

    def cut(i):
        return pl.ds(pl.multiple_of(i * TILE, TILE), TILE)

    def prepare(i, carry):
        span = cut(i)
        rows = lax.broadcasted_iota(jnp.int32, (onehot.shape[0], TILE), 0)
        onehot[:, span] = jnp.where(rows == lead[0:1, span], 1.0, 0.0).astype(BF16)
        rows = lax.broadcasted_iota(jnp.int32, (atoms, TILE), 0)
        onehot_c[:, span] = jnp.where(rows == lead[1:2, span], 1.0, 0.0).astype(BF16)
        pre = mm(rad0_t, basis[:, span].astype(BF16))
        sig = jax.nn.sigmoid(pre)
        slope[:, span] = sig * (1.0 + pre * (1.0 - sig))
        hidden = (pre * sig).astype(BF16)
        rad1[:, span] = mm(rad1_t1, hidden[:hid])
        rad2[:, span] = mm(rad1_t2, hidden[hid:])
        return carry

    lax.fori_loop(0, tiles, prepare, 0)

    spread_finish(kinds, kinds_first)
    ghost_kinds = mm_nt(eye(16, kinds.shape[1]), kinds[...]).astype(BF16)
    agg[...] = jnp.zeros_like(agg)

    def layer_one(i, carry):
        span = cut(i)
        kind = mm(kind_t[:16], onehot[pl.ds(0, atoms), span]) + mm(
            ghost_kinds, onehot[pl.ds(atoms, ghosts), span]
        )
        proj = mm(kind_proj, kind.astype(BF16))
        proj1[:, span] = proj
        lead_s = proj[:width] * rad1[pl.ds(0, width), span]
        lead_t = proj[width:] * rad1[pl.ds(width, chan), span]
        parts = [lead_s.astype(BF16)]
        for m in range(8):
            parts.append((lead_t * harm[pl.ds(m, 1), span]).astype(BF16))
        agg[...] += mm_nt(jnp.concatenate(parts, axis=0), onehot_c[:, span])
        return carry

    lax.fori_loop(0, tiles, layer_one, 0)
    gathered = 0.25 * agg[...]
    gathered_t = gathered[width:]
    rounded = gathered[:width].astype(BF16)
    pre1 = mm(out1_t, rounded)
    sig1 = jax.nn.sigmoid(pre1)
    gate = jax.nn.sigmoid(mm(gate_t, rounded))
    scalars = (start + pre1 * sig1).astype(BF16)
    gates = jnp.concatenate([gate] * 8, axis=0)
    tensors = (gathered_t * gates).astype(BF16)
    proj2 = mm(src2_t, scalars).astype(BF16)
    local = jnp.concatenate([proj2[:width], tensors], axis=0)
    halo[pl.ds(own_row, sends), :] = mm_nt(lend, local).astype(BF16)
    halo_first = spread_start(halo)
    table[:, pl.ds(0, atoms)] = local
    spread_finish(halo, halo_first)
    table[:, pl.ds(atoms, ghosts)] = halo[...].T
    agg2[...] = jnp.zeros_like(agg2)

    def layer_two(i, carry):
        span = cut(i)
        rows = mm(table[...], onehot[pl.ds(0, atoms + ghosts), span])
        picked[:, span] = rows.astype(BF16)
        inner = jnp.zeros((chan, TILE), F32)
        for m in range(8):
            inner += rows[width + m * chan : width + (m + 1) * chan] * harm[pl.ds(m, 1), span]
        message = rows[:width] * rad2[:, span] + mm(inv_t, inner.astype(BF16))
        agg2[...] += mm_nt(message.astype(BF16), onehot_c[:, span])
        return carry

    lax.fori_loop(0, tiles, layer_two, 0)
    rounded = (0.25 * agg2[...]).astype(BF16)
    pre2 = mm(out2_t, rounded)
    sig2 = jax.nn.sigmoid(pre2)
    readout = jnp.broadcast_to(w_energy[...], (width, width)).T[:, :1]
    mask = jnp.where(
        lax.broadcasted_iota(jnp.int32, (1, atoms), 1) < atom_count[0, 0], 1.0, 0.0
    )
    energies[...] = mask * sum_rows((scalars.astype(F32) + pre2 * sig2) * readout)

    d_new = readout * mask
    d_pre = (d_new * sig2 * (1.0 + pre2 * (1.0 - sig2))).astype(BF16)
    d_agg = (0.25 * mm(w_out[1], d_pre).astype(BF16).astype(F32)).astype(BF16)

    def back_two(i, carry):
        span = cut(i)
        d_msg = mm(d_agg, onehot_c[:, span])
        dmsg[pl.ds(0, width), span] = (d_msg * rad2[:, span]).astype(BF16)
        d_inv = mm(w_inv[1], d_msg.astype(BF16))
        for m in range(8):
            dmsg[pl.ds(width + m * chan, chan), span] = (d_inv * harm[pl.ds(m, 1), span]).astype(BF16)
        return carry

    lax.fori_loop(0, tiles, back_two, 0)
    back_y = []
    for slot, part, by in ((0, 0, -1), (1, 2, 1)):
        back_send_y[slot] = mm_nt(
            onehot[pl.ds(atoms + part * rows_y, rows_y), :], dmsg[...]
        ).astype(BF16)
        back_y.append(send(back_send_y.at[slot], back_recv_y.at[slot], "gy", by))
    back = mm_nt(onehot[pl.ds(atoms + rows_y, rows_y), :], dmsg[...])
    d_local = mm_nt(dmsg[...], onehot[pl.ds(0, atoms), :])

    def edge_two(i, carry):
        span = cut(i)
        d_msg = mm(d_agg, onehot_c[:, span])
        d_inv = mm(w_inv[1], d_msg.astype(BF16))
        for m in range(8):
            grad_y[pl.ds(m, 1), span] = sum_rows(
                d_inv * picked[pl.ds(width + m * chan, chan), span].astype(F32)
            )
        d_rad = (d_msg * picked[pl.ds(0, width), span].astype(F32)).astype(BF16)
        d_hid = mm(w_rad1[1][:, :width], d_rad) * slope[pl.ds(hid, hid), span]
        d_bas = mm(w_rad0[1], d_hid.astype(BF16))
        grad_d[:, span] = sum_rows(d_bas * dbas[:, span])
        return carry

    lax.fori_loop(0, tiles, edge_two, 0)
    for copy in back_y:
        copy.wait_recv()
    back = back + back_recv_y[0].astype(F32) + back_recv_y[1].astype(F32)
    back_x = []
    for slot, part, by in ((0, 0, -1), (1, 2, 1)):
        back_send_x[slot] = back[part * rows_x : (part + 1) * rows_x].astype(BF16)
        back_x.append(send(back_send_x.at[slot], back_recv_x.at[slot], "gx", by))
    back = back[rows_x : 2 * rows_x]
    for copy in back_x:
        copy.wait_recv()
    back = back + back_recv_x[0].astype(F32) + back_recv_x[1].astype(F32)
    back_z = []
    for slot, part, by in ((0, 0, -1), (1, 2, 1)):
        back_send_z[slot] = back[part * sends : (part + 1) * sends].astype(BF16)
        back_z.append(send(back_send_z.at[slot], back_recv_z.at[slot], "gz", by))
    back = back[sends : 2 * sends]
    for copy in back_z:
        copy.wait_recv()
    back = back + back_recv_z[0].astype(F32) + back_recv_z[1].astype(F32)
    owned = d_local + mm(back.T.astype(BF16), lend)

    d_scalars = (d_new + mm(w_src[1][:, :width], owned[:width].astype(BF16))).astype(BF16).astype(F32)
    d_tensors = owned[width:].astype(BF16).astype(F32)
    d_pre = (d_scalars * sig1 * (1.0 + pre1 * (1.0 - sig1))).astype(BF16)
    product = d_tensors * gathered_t
    d_gate = jnp.zeros((chan, atoms), F32)
    for m in range(8):
        d_gate += product[m * chan : (m + 1) * chan]
    d_gate = (d_gate * gate * (1.0 - gate)).astype(BF16)
    d_scalar_agg = (mm(w_out[0], d_pre) + mm(w_gate[0], d_gate)).astype(BF16).astype(F32)
    d_agg1 = (0.25 * jnp.concatenate([d_scalar_agg, d_tensors * gates], axis=0)).astype(BF16)

    def edge_one(i, carry):
        span = cut(i)
        d_msg = mm(d_agg1, onehot_c[:, span])
        proj = proj1[:, span]
        lead_t = proj[width:] * rad1[pl.ds(width, chan), span]
        inner = jnp.zeros((chan, TILE), F32)
        gy = []
        for m in range(8):
            d_part = d_msg[width + m * chan : width + (m + 1) * chan]
            inner += d_part * harm[pl.ds(m, 1), span]
            gy.append(grad_y[pl.ds(m, 1), span] + sum_rows(d_part * lead_t))
        d_rad = jnp.concatenate([d_msg[:width], inner], axis=0) * proj
        d_hid = mm(w_rad1[0][:, : width + chan], d_rad.astype(BF16)) * slope[pl.ds(0, hid), span]
        d_bas = mm(w_rad0[0], d_hid.astype(BF16))
        gd = grad_d[:, span] + sum_rows(d_bas * dbas[:, span])
        ax, ay, az = geo[0:1, span], geo[1:2, span], geo[2:3, span]
        gux = gy[0] + root * (ay * gy[3] + az * gy[6] + ax * gy[7])
        guy = gy[1] + root * (ax * gy[3] + az * gy[4] - ay * gy[7])
        guz = gy[2] + root * (ay * gy[4] + ax * gy[6]) + 3.0 * az * gy[5]
        radial = gd - geo[3:4, span] * (ax * gux + ay * guy + az * guz)
        pull[pl.ds(0, 1), span] = geo[3:4, span] * gux + ax * radial
        pull[pl.ds(1, 1), span] = geo[3:4, span] * guy + ay * radial
        pull[pl.ds(2, 1), span] = geo[3:4, span] * guz + az * radial
        return carry

    pull[...] = jnp.zeros_like(pull)
    lax.fori_loop(0, tiles, edge_one, 0)

    halves = split(pull[...])

    def slab(part_b, part_a):
        first = atoms + part_b * rows_y + part_a * rows_x
        return joined(mm_nt(halves, onehot[pl.ds(first, 128), :]))

    f_y = []
    for slot, part, by in ((0, 0, -1), (1, 2, 1)):
        for a in range(3):
            f_send_y[slot, :, pl.ds(a * 128, 128)] = slab(part, a)
        f_y.append(send(f_send_y.at[slot], f_recv_y.at[slot], "gy", by))
    total = joined(mm_nt(halves, onehot_c[...])) - joined(mm_nt(halves, onehot[pl.ds(0, atoms), :]))
    sums = [slab(1, a) for a in range(3)]
    for copy in f_y:
        copy.wait_recv()
    sums = [
        sums[a] + f_recv_y[0, :, pl.ds(a * 128, 128)] + f_recv_y[1, :, pl.ds(a * 128, 128)] for a in range(3)
    ]
    f_x = []
    for slot, part, by in ((0, 0, -1), (1, 2, 1)):
        f_send_x[slot] = sums[part]
        f_x.append(send(f_send_x.at[slot], f_recv_x.at[slot], "gx", by))
    for copy in f_x:
        copy.wait_recv()
    plane = sums[1] + f_recv_x[0] + f_recv_x[1]
    f_send_z[...] = plane
    f_z = [
        send(f_send_z, f_recv_z.at[0], "gz", -1),
        send(f_send_z, f_recv_z.at[1], "gz", 1),
    ]
    for copy in f_z:
        copy.wait_recv()
    plane = (
        pltpu.roll(plane, 128 - sends, 1) + f_recv_z[0] + pltpu.roll(f_recv_z[1], 128 - 2 * sends, 1)
    )
    lend_wide = mm_nt(eye(128, sends), lend_t).astype(BF16)
    total = total - joined(mm(split(plane), lend_wide))
    forces[...] = total[:3]
    for copy in started:
        copy.wait_send()


def per_device(
    species, atom_count, send_list, edge_count, edge_center, edge_neighbour, edge_vectors,
    embed, w_src, w_rad0, w_rad1, w_inv, w_out, w_gate, w_energy,
):
    atoms = species.shape[-1]
    edges = edge_center.shape[-1]
    sends = send_list.shape[-1]
    width = w_out.shape[1]
    chan = w_gate.shape[2]
    hid = w_rad0.shape[2]
    cols = width + 8 * chan
    ghosts = 27 * sends
    vmem = pl.BlockSpec(memory_space=pltpu.VMEM)
    smem = pl.BlockSpec(memory_space=pltpu.SMEM)
    copies = 10 + 10 + 6 + 6
    energies, forces = pl.pallas_call(
        body,
        out_shape=(
            jax.ShapeDtypeStruct((1, atoms), F32),
            jax.ShapeDtypeStruct((3, atoms), F32),
        ),
        in_specs=[smem, smem] + [vmem] * 13,
        out_specs=(vmem, vmem),
        scratch_shapes=[
            pltpu.VMEM((1024, edges), BF16),
            pltpu.VMEM((atoms, edges), BF16),
            pltpu.VMEM((ghosts, 128), BF16),
            pltpu.VMEM((ghosts, cols), BF16),
            pltpu.VMEM((cols, atoms + ghosts), BF16),
            pltpu.VMEM((cols, edges), BF16),
            pltpu.VMEM((cols, edges), BF16),
            pltpu.VMEM((8, edges), F32),
            pltpu.VMEM((8, edges), F32),
            pltpu.VMEM((8, edges), F32),
            pltpu.VMEM((16, edges), F32),
            pltpu.VMEM((2 * hid, edges), F32),
            pltpu.VMEM((width + chan, edges), F32),
            pltpu.VMEM((width, edges), F32),
            pltpu.VMEM((width + chan, edges), F32),
            pltpu.VMEM((8, edges), jnp.int32),
            pltpu.VMEM((cols, atoms), F32),
            pltpu.VMEM((width, atoms), F32),
            pltpu.VMEM((8, edges), F32),
            pltpu.VMEM((1, edges), F32),
            pltpu.VMEM((8, edges), F32),
            pltpu.VMEM((2, 9 * sends, cols), BF16),
            pltpu.VMEM((2, 9 * sends, cols), BF16),
            pltpu.VMEM((2, 3 * sends, cols), BF16),
            pltpu.VMEM((2, 3 * sends, cols), BF16),
            pltpu.VMEM((2, sends, cols), BF16),
            pltpu.VMEM((2, sends, cols), BF16),
            pltpu.VMEM((2, 8, 384), F32),
            pltpu.VMEM((2, 8, 384), F32),
            pltpu.VMEM((2, 8, 128), F32),
            pltpu.VMEM((2, 8, 128), F32),
            pltpu.VMEM((8, 128), F32),
            pltpu.VMEM((2, 8, 128), F32),
            pltpu.SemaphoreType.DMA((copies,)),
            pltpu.SemaphoreType.DMA((copies,)),
        ],
        compiler_params=pltpu.CompilerParams(
            collective_id=0, has_side_effects=True, vmem_limit_bytes=52 * 1024 * 1024
        ),
    )(
        atom_count.reshape(1, 1), edge_count.reshape(1, 1), species.reshape(1, atoms),
        send_list.reshape(1, sends), edge_center.reshape(1, edges), edge_neighbour.reshape(1, edges),
        edge_vectors.reshape(3, edges), embed, w_src, w_rad0, w_rad1, w_inv, w_out, w_gate,
        w_energy.reshape(1, width),
    )
    return energies.reshape(species.shape), forces.reshape(edge_vectors.shape[:3] + (3, atoms))


def solution(mesh):
    shard = P("gx", "gy", "gz", None)
    count = P("gx", "gy", "gz")
    wide = P("gx", "gy", "gz", None, None)
    return jax.shard_map(
        per_device,
        mesh=mesh,
        in_specs=(shard, count, shard, count, shard, shard, wide) + (P(),) * 8,
        out_specs=(shard, wide),
        check_vma=False,
    )
```

profile of v0, /device:TPU:1, one launch (start us, length us, event | category | flops | bytes accessed | tf_op | source)
XLA Modules:
  0.0 96.6 jit_solution(8676206666370609374)
XLA Ops:
  0.6 0.0 copy-start.10
  2.0 0.8 copy.22
  2.7 0.9 copy.18.w_gate
  3.6 0.0 copy-done.10
  3.6 0.0 copy-start
  3.6 0.0 copy-start.1
  3.6 0.0 copy-start.2
  3.7 0.0 copy-start.3
  3.7 0.0 copy-start.4
  3.7 0.0 copy-start.5
  3.7 0.0 copy-start.6
  3.7 0.0 copy-start.7
  3.7 0.0 copy-start.8
  3.7 0.0 copy-start.9
  3.7 0.1 copy.17.w_src
  3.9 0.6 copy-done
  4.5 0.0 copy-done.1
  4.5 0.0 copy-done.2
  4.5 0.0 copy-done.3
  4.5 0.0 copy-done.4
  4.5 0.0 copy-done.5
  4.5 91.0 %shard_map.158 = (f32[1,128]{1,0:T(1,128)S(1)}, f32[3,128]{1,0:T(4,128)S(1)}) custom-call(s32[1,1]{1,0:T(1,128)} %bitcast.12.atom_count, s32[1,1]{1,0:T(1,128)} %bitcast.13.edge_count, s32[1,128]{1,0:T(1,128)S(1)} %bitcast.18, s32[1,32]{1,0:T(1,128)S(1)} %bitcast.19, s32[1,2560]{1,0:T(1,128)S(1)} %bitcast.15, s32[1,2560]{1,0:T(1,128)S(1)} %bitcast.16, ...), custom_call_target="tpu_custom_call" | custom-call | tf_op jit(solution)/shard_map/pallas_call | solution.py:437
  95.6 0.6 copy.19
  96.1 0.5 copy.26
  (4 shorter events, 0.0 us)
Async XLA Ops:
  0.6 3.0 %copy-start.10 = (bf16[2,128,192]{1,2,0:T(8,128)(2,1)S(1)}, bf16[2,128,192]{1,2,0:T(8,128)(2,1)}, u32[]{:S(2)}) copy-start(bf16[2,128,192]{1,2,0:T(8,128)(2,1)} %param.23) | copy-start | bytes 294916
  3.6 0.8 copy-start
  3.6 0.9 copy-start.1
  3.6 0.9 copy-start.2
  3.7 0.8 copy-start.3
  3.7 0.8 copy-start.4
  3.7 0.8 copy-start.5
  3.7 0.8 copy-start.6
  3.7 0.8 copy-start.7
  3.7 0.8 copy-start.8
  3.7 0.8 copy-start.9
where the time goes:
time: 96.9 us; the launch traced here: 96.6 us
  Pallas kernels  91 us (94%)
  local copies, waits for them, and re-layouts  3.52 us (4%)
  between operations  2.11 us (2%)
    pallas_call x1, Pallas kernels, per_device(): pl.pallas_call(body, out_shape=(jax.ShapeDtypeStruct((1, atoms), F32), ja...  91 us
    unnamed x27, local copies, waits for them, and re-layouts  3.52 us

commit v1 on v0

v1 whole, which is shorter than its diff:
```python
import functools
import math

import jax
import jax.numpy as jnp
from jax import lax
from jax.experimental import pallas as pl
from jax.experimental.pallas import tpu as pltpu
from jax.sharding import PartitionSpec as P

RADIAL = 8
CUTOFF = 5.0
TILE = 1280
MESH = pl.DeviceIdType.MESH
BF16 = jnp.bfloat16
F32 = jnp.float32


def mm(left, right):
    return lax.dot_general(left, right, (((1,), (0,)), ((), ())), preferred_element_type=F32)


def mm_nt(left, right):
    return lax.dot_general(left, right, (((1,), (1,)), ((), ())), preferred_element_type=F32)


def eye(rows, cols):
    first = lax.broadcasted_iota(jnp.int32, (rows, cols), 0)
    second = lax.broadcasted_iota(jnp.int32, (rows, cols), 1)
    return jnp.where(first == second, 1.0, 0.0).astype(BF16)


def turned(array):
    return mm_nt(eye(array.shape[1], array.shape[1]), array).astype(BF16)


def split(array):
    high = array.astype(BF16).astype(F32)
    return jnp.concatenate([high, array - high], axis=0).astype(BF16)


def joined(array):
    half = array.shape[0] // 2
    return array[:half] + array[half:]


def sum_rows(array):
    return jnp.sum(array, axis=0, keepdims=True)


def sin_cos(angle):
    y = angle - (math.pi / 2)
    y2 = y * y
    sin_y = jnp.full_like(y, -1.0 / math.factorial(11))
    for power in (9, 7, 5, 3, 1):
        sin_y = sin_y * y2 + ((-1.0) ** (power // 2)) / math.factorial(power)
    cos_y = jnp.full_like(y, 1.0 / math.factorial(12))
    for power in (10, 8, 6, 4, 2, 0):
        cos_y = cos_y * y2 + ((-1.0) ** (power // 2)) / math.factorial(power)
    return cos_y, -(sin_y * y)


def body(
    atom_count, edge_count, *refs
):
    args, (energies, forces), held = refs[:13], refs[13:15], refs[15:28]
    (
        onehot, onehot_c, block_of, slot_of, kinds, halo, table, picked, dmsg,
        geo, harm, dbas, basis, slope, rad1, rad2, proj1, agg, agg2, grad_y, grad_d, pull,
        back_send_y, back_recv_y, back_send_x, back_recv_x, back_send_z, back_recv_z,
        f_all, f_recv_y, f_send_x, f_recv_x, f_send_z, f_recv_z,
        send_sems, recv_sems, arg_sems,
    ) = refs[28:]
    (
        species, send_list, vectors, neighbour, center,
        embed, w_src, w_rad0, w_rad1, w_inv, w_out, w_gate, w_energy,
    ) = held
    atoms = species.shape[1]
    edges = center.shape[1]
    sends = send_list.shape[1]
    width = w_out.shape[1]
    chan = w_gate.shape[1]
    rows_x = 3 * sends
    rows_y = 9 * sends
    ghosts = 27 * sends
    tiles = edges // TILE
    unit = 8
    blocks = atoms // sends + 27

    def step(axis, by):
        size = lax.axis_size(axis)
        return {axis: lax.rem(lax.axis_index(axis) + size + by, size)}

    barrier = pltpu.get_barrier_semaphore()
    for axis in ("gx", "gy", "gz"):
        for by in (1, -1):
            pl.semaphore_signal(barrier, inc=1, device_id=step(axis, by), device_id_type=MESH)

    loads = [
        pltpu.make_async_copy(source, target, arg_sems.at[i])
        for i, (source, target) in enumerate(zip(args, held))
    ]
    for load in loads:
        load.start()

    next_sem = [0]
    started = []

    def send(source, target, axis, by):
        slot = next_sem[0]
        next_sem[0] = slot + 1
        copy = pltpu.make_async_remote_copy(
            src_ref=source, dst_ref=target, send_sem=send_sems.at[slot], recv_sem=recv_sems.at[slot],
            device_id=step(axis, by), device_id_type=MESH,
        )
        copy.start()
        started.append(copy)
        return copy

    def spread(ref, size, between):
        def at(b, a, c):
            return ref.at[pl.ds(((b * 3 + a) * 3 + c) * size, size)]

        def along(axis, b, a, c):
            sides = {"gz": ((b, a, 0), (b, a, 2)), "gx": ((b, 0, c), (b, 2, c)), "gy": ((0, a, c), (2, a, c))}
            return [send(at(b, a, c), at(*side), axis, by) for side, by in zip(sides[axis], (1, -1))]

        def arrived(copies):
            for copy in copies:
                copy.wait_recv()

        in_z = along("gz", 1, 1, 1)
        in_x = along("gx", 1, 1, 1)
        in_y = along("gy", 1, 1, 1)
        between[0]()
        arrived(in_x)
        in_y += along("gy", 1, 0, 1) + along("gy", 1, 2, 1)
        arrived(in_z)
        in_x = along("gx", 1, 1, 0) + along("gx", 1, 1, 2)
        in_y += along("gy", 1, 1, 0) + along("gy", 1, 1, 2)
        between[1]()
        arrived(in_x)
        for c in (0, 2):
            in_y += along("gy", 1, 0, c) + along("gy", 1, 2, c)
        between[2]()
        arrived(in_y)

    loads[0].wait()
    loads[1].wait()
    lane = lax.broadcasted_iota(jnp.int32, (atoms, atoms), 0)
    kind_t = jnp.where(lane == species[...], 1.0, 0.0).astype(BF16)
    lend_t = jnp.where(
        lax.broadcasted_iota(jnp.int32, (atoms, sends), 0) == send_list[...], 1.0, 0.0
    ).astype(BF16)
    lend_wide = mm_nt(eye(128, sends), lend_t).astype(BF16)
    lend = lend_wide[:sends]
    species_rows = jnp.broadcast_to(species[...].astype(F32), (unit, atoms))
    kinds[pl.ds(13 * unit, unit), :] = mm_nt(species_rows.astype(BF16), lend_wide)
    pl.semaphore_wait(barrier, 6)

    def geometry():
        for load in loads[2:5]:
            load.wait()
        live = lax.broadcasted_iota(jnp.int32, (1, edges), 1) < edge_count[0, 0, 0]
        x = jnp.where(live, vectors[0], 1.0)
        y = jnp.where(live, vectors[1], 1.0)
        z = jnp.where(live, vectors[2], 1.0)
        square = x * x + y * y + z * z
        inverse = lax.rsqrt(square)
        distance = square * inverse
        ux, uy, uz = x * inverse, y * inverse, z * inverse
        for row, value in enumerate((ux, uy, uz, inverse)):
            geo[pl.ds(row, 1), :] = value
        for row, value in enumerate((
            ux, uy, uz, root * ux * uy, root * uy * uz, 0.5 * (3.0 * uz * uz - 1.0), root * ux * uz,
            0.5 * root * (ux * ux - uy * uy),
        )):
            harm[pl.ds(row, 1), :] = value
        sine, cosine = sin_cos(distance * (math.pi / CUTOFF))
        ratio = distance * (1.0 / CUTOFF)
        rest = 1.0 - ratio * ratio
        scale = rest * rest * inverse
        dscale = -(4.0 / CUTOFF) * rest * ratio * inverse - scale * inverse
        sin_k, cos_k = sine, cosine
        basis[...] = jnp.zeros_like(basis)
        for k in range(1, RADIAL + 1):
            basis[pl.ds(k - 1, 1), :] = sin_k * scale
            dbas[pl.ds(k - 1, 1), :] = (k * math.pi / CUTOFF) * cos_k * scale + sin_k * dscale
            sin_k, cos_k = sin_k * cosine + cos_k * sine, cos_k * cosine - sin_k * sine

        near = neighbour[...]
        ghost = near - atoms
        part_a = jnp.where(ghost >= rows_y, 1, 0) + jnp.where(ghost >= 2 * rows_y, 1, 0)
        ghost = ghost - rows_y * part_a
        part_b = jnp.where(ghost >= rows_x, 1, 0) + jnp.where(ghost >= 2 * rows_x, 1, 0)
        ghost = ghost - rows_x * part_b + rows_x * part_a + rows_y * part_b + atoms
        place = jnp.where(live, jnp.where(near < atoms, near, ghost), -1)
        middle = jnp.where(live, center[...], -1)
        block = lax.shift_right_arithmetic(place, sends.bit_length() - 1)
        slot = lax.bitwise_and(place, sends - 1)
        rows = lax.broadcasted_iota(jnp.int32, (32, edges), 0)
        block_of[...] = jnp.where(rows == block, 1.0, 0.0).astype(BF16)
        rows = lax.broadcasted_iota(jnp.int32, (atoms, edges), 0)
        slot_of[...] = jnp.where(rows == slot, 1.0, 0.0).astype(BF16)
        onehot_c[...] = jnp.where(rows == middle, 1.0, 0.0).astype(BF16)
        rows = lax.broadcasted_iota(jnp.int32, onehot.shape, 0)
        onehot[...] = jnp.where(rows == place, 1.0, 0.0).astype(BF16)

    def cut(i):
        return pl.ds(pl.multiple_of(i * TILE, TILE), TILE)

    def radial():
        for load in loads[5:]:
            load.wait()
        rad0_t = jnp.concatenate(
            [
                turned(
                    jnp.concatenate(
                        [w_rad0[l].astype(F32), jnp.zeros((8, w_rad0.shape[2]), F32)], axis=0
                    ).astype(BF16)
                ).astype(F32)
                for l in range(2)
            ],
            axis=0,
        ).astype(BF16)
        rad1_t1 = turned(w_rad1[0][:, : width + chan])
        rad1_t2 = turned(w_rad1[1][:, :width])

        def prepare(i, carry):
            span = cut(i)
            pre = mm(rad0_t, basis[:, span].astype(BF16))
            sig = jax.nn.sigmoid(pre)
            slope[:, span] = sig * (1.0 + pre * (1.0 - sig))
            hidden = (pre * sig).astype(BF16)
            rad1[:, span] = mm(rad1_t1, hidden[:hid])
            rad2[:, span] = mm(rad1_t2, hidden[hid:])
            return carry

        lax.fori_loop(0, tiles, prepare, 0)

    root = math.sqrt(3.0)
    hid = w_rad0.shape[2]
    spread(kinds, unit, (geometry, radial, lambda: None))
    src1_t = w_src[0]
    src2_t = w_src[1]
    src2 = turned(src2_t[:width])
    inv_t = turned(w_inv[1])
    out1_t = turned(w_out[0])
    out2_t = turned(w_out[1])
    gate_t = w_gate[0]
    embed_rows = jnp.concatenate([embed[...], jnp.zeros((16 - embed.shape[0], width), F32)], axis=0)
    embed_t = turned(embed_rows.astype(BF16))
    kind_proj = mm(src1_t, embed_t).astype(BF16)
    start = mm(embed_t, kind_t[:16, :])

    number = species_rows[:1]
    kind_rows = [number] + [pltpu.roll(number, atoms - j * sends, 1) for j in range(1, atoms // sends)]
    kind_rows += [kinds[pl.ds(i * unit, 1), :] for i in range(27)]
    kind_rows += [jnp.zeros((1, atoms), F32)] * (32 - blocks)
    kind_table = mm_nt(eye(sends, atoms), jnp.concatenate(kind_rows, axis=0).astype(BF16)).astype(BF16)
    agg[...] = jnp.zeros_like(agg)

    def layer_one(i, carry):
        span = cut(i)
        kind = sum_rows(mm(kind_table, block_of[:, span]) * slot_of[pl.ds(0, sends), span].astype(F32))
        kind_ids = lax.broadcasted_iota(jnp.int32, (16, TILE), 0).astype(F32)
        proj = mm(kind_proj, jnp.where(kind_ids == kind, 1.0, 0.0).astype(BF16))
        proj1[:, span] = proj
        lead_s = proj[:width] * rad1[pl.ds(0, width), span]
        lead_t = proj[width:] * rad1[pl.ds(width, chan), span]
        parts = [lead_s.astype(BF16)]
        for m in range(8):
            parts.append((lead_t * harm[pl.ds(m, 1), span]).astype(BF16))
        agg[...] += mm_nt(jnp.concatenate(parts, axis=0), onehot_c[:, span])
        return carry

    lax.fori_loop(0, tiles, layer_one, 0)
    gathered = 0.25 * agg[...]
    gathered_t = gathered[width:]
    rounded = gathered[:width].astype(BF16)
    pre1 = mm(out1_t, rounded)
    sig1 = jax.nn.sigmoid(pre1)
    gate = jax.nn.sigmoid(mm(gate_t, rounded))
    scalars = (start + pre1 * sig1).astype(BF16)
    gates = jnp.concatenate([gate] * 8, axis=0)
    tensors = (gathered_t * gates).astype(BF16)
    proj2 = mm(src2_t, scalars).astype(BF16)
    local = jnp.concatenate([proj2[:width], tensors], axis=0)
    halo[pl.ds(13 * sends, sends), :] = mm_nt(lend, local).astype(BF16)
    table[:, pl.ds(0, atoms)] = local
    nothing = lambda: None
    spread(halo, sends, (nothing, nothing, nothing))
    table[:, pl.ds(atoms, ghosts)] = halo[...].T
    agg2[...] = jnp.zeros_like(agg2)

    def layer_two(i, carry):
        span = cut(i)
        rows = mm(table[...], onehot[pl.ds(0, atoms + ghosts), span])
        picked[:, span] = rows.astype(BF16)
        inner = jnp.zeros((chan, TILE), F32)
        for m in range(8):
            inner += rows[width + m * chan : width + (m + 1) * chan] * harm[pl.ds(m, 1), span]
        message = rows[:width] * rad2[:, span] + mm(inv_t, inner.astype(BF16))
        agg2[...] += mm_nt(message.astype(BF16), onehot_c[:, span])
        return carry

    lax.fori_loop(0, tiles, layer_two, 0)
    rounded = (0.25 * agg2[...]).astype(BF16)
    pre2 = mm(out2_t, rounded)
    sig2 = jax.nn.sigmoid(pre2)
    readout = jnp.broadcast_to(w_energy[...], (width, width)).T[:, :1]
    mask = jnp.where(
        lax.broadcasted_iota(jnp.int32, (1, atoms), 1) < atom_count[0, 0, 0], 1.0, 0.0
    )
    energies[...] = mask * sum_rows((scalars.astype(F32) + pre2 * sig2) * readout)

    d_new = readout * mask
    d_pre = (d_new * sig2 * (1.0 + pre2 * (1.0 - sig2))).astype(BF16)
    d_agg = (0.25 * mm(w_out[1], d_pre).astype(BF16).astype(F32)).astype(BF16)

    def back_two(i, carry):
        span = cut(i)
        d_msg = mm(d_agg, onehot_c[:, span])
        dmsg[pl.ds(0, width), span] = (d_msg * rad2[:, span]).astype(BF16)
        d_inv = mm(w_inv[1], d_msg.astype(BF16))
        for m in range(8):
            dmsg[pl.ds(width + m * chan, chan), span] = (d_inv * harm[pl.ds(m, 1), span]).astype(BF16)
        return carry

    lax.fori_loop(0, tiles, back_two, 0)
    back_y = {}
    for slot, part, by in ((0, 0, -1), (1, 2, 1)):
        back_send_y[slot] = mm_nt(
            onehot[pl.ds(atoms + part * rows_y, rows_y), :], dmsg[...]
        ).astype(BF16)
        for a in (0, 2, 1):
            rows = pl.ds(a * rows_x, rows_x)
            back_y[slot, a] = send(back_send_y.at[slot, rows], back_recv_y.at[slot, rows], "gy", by)
    back = mm_nt(onehot[pl.ds(atoms + rows_y, rows_y), :], dmsg[...])
    d_local = mm_nt(dmsg[...], onehot[pl.ds(0, atoms), :])

    def edge_two(i, carry):
        span = cut(i)
        d_msg = mm(d_agg, onehot_c[:, span])
        d_inv = mm(w_inv[1], d_msg.astype(BF16))
        for m in range(8):
            grad_y[pl.ds(m, 1), span] = sum_rows(
                d_inv * picked[pl.ds(width + m * chan, chan), span].astype(F32)
            )
        d_rad = (d_msg * picked[pl.ds(0, width), span].astype(F32)).astype(BF16)
        d_hid = mm(w_rad1[1][:, :width], d_rad) * slope[pl.ds(hid, hid), span]
        d_bas = mm(w_rad0[1], d_hid.astype(BF16))
        grad_d[:, span] = sum_rows(d_bas * dbas[:, span])
        return carry

    lax.fori_loop(0, tiles, edge_two, 0)

    def merged(a):
        rows = pl.ds(a * rows_x, rows_x)
        for slot in range(2):
            back_y[slot, a].wait_recv()
        return (
            back[a * rows_x : (a + 1) * rows_x] + back_recv_y[0, rows].astype(F32) + back_recv_y[1, rows].astype(F32)
        )

    back_x = {}
    for slot, part, by in ((0, 0, -1), (1, 2, 1)):
        back_send_x[slot] = merged(part).astype(BF16)
        for c in (0, 2, 1):
            rows = pl.ds(c * sends, sends)
            back_x[slot, c] = send(back_send_x.at[slot, rows], back_recv_x.at[slot, rows], "gx", by)
    middle_rows = merged(1)

    def gathered_x(c):
        rows = pl.ds(c * sends, sends)
        for slot in range(2):
            back_x[slot, c].wait_recv()
        return (
            middle_rows[c * sends : (c + 1) * sends]
            + back_recv_x[0, rows].astype(F32) + back_recv_x[1, rows].astype(F32)
        )

    back_z = []
    for slot, part, by in ((0, 0, -1), (1, 2, 1)):
        back_send_z[slot] = gathered_x(part).astype(BF16)
        back_z.append(send(back_send_z.at[slot], back_recv_z.at[slot], "gz", by))
    back = gathered_x(1)
    for copy in back_z:
        copy.wait_recv()
    back = back + back_recv_z[0].astype(F32) + back_recv_z[1].astype(F32)
    owned = d_local + mm(back.T.astype(BF16), lend)

    d_scalars = (d_new + mm(src2, owned[:width].astype(BF16))).astype(BF16).astype(F32)
    d_tensors = owned[width:].astype(BF16).astype(F32)
    d_pre = (d_scalars * sig1 * (1.0 + pre1 * (1.0 - sig1))).astype(BF16)
    product = d_tensors * gathered_t
    d_gate = jnp.zeros((chan, atoms), F32)
    for m in range(8):
        d_gate += product[m * chan : (m + 1) * chan]
    d_gate = (d_gate * gate * (1.0 - gate)).astype(BF16)
    d_scalar_agg = (mm(w_out[0], d_pre) + mm(turned(gate_t), d_gate)).astype(BF16).astype(F32)
    d_agg1 = (0.25 * jnp.concatenate([d_scalar_agg, d_tensors * gates], axis=0)).astype(BF16)

    def edge_one(i, carry):
        span = cut(i)
        d_msg = mm(d_agg1, onehot_c[:, span])
        proj = proj1[:, span]
        lead_t = proj[width:] * rad1[pl.ds(width, chan), span]
        inner = jnp.zeros((chan, TILE), F32)
        gy = []
        for m in range(8):
            d_part = d_msg[width + m * chan : width + (m + 1) * chan]
            inner += d_part * harm[pl.ds(m, 1), span]
            gy.append(grad_y[pl.ds(m, 1), span] + sum_rows(d_part * lead_t))
        d_rad = jnp.concatenate([d_msg[:width], inner], axis=0) * proj
        d_hid = mm(w_rad1[0][:, : width + chan], d_rad.astype(BF16)) * slope[pl.ds(0, hid), span]
        d_bas = mm(w_rad0[0], d_hid.astype(BF16))
        gd = grad_d[:, span] + sum_rows(d_bas * dbas[:, span])
        ax, ay, az = geo[0:1, span], geo[1:2, span], geo[2:3, span]
        gux = gy[0] + root * (ay * gy[3] + az * gy[6] + ax * gy[7])
        guy = gy[1] + root * (ax * gy[3] + az * gy[4] - ay * gy[7])
        guz = gy[2] + root * (ay * gy[4] + ax * gy[6]) + 3.0 * az * gy[5]
        radial = gd - geo[3:4, span] * (ax * gux + ay * guy + az * guz)
        pull[pl.ds(0, 1), span] = geo[3:4, span] * gux + ax * radial
        pull[pl.ds(1, 1), span] = geo[3:4, span] * guy + ay * radial
        pull[pl.ds(2, 1), span] = geo[3:4, span] * guz + az * radial
        return carry

    pull[...] = jnp.zeros_like(pull)
    lax.fori_loop(0, tiles, edge_one, 0)

    pulls = pull[...]
    high = pulls.astype(BF16).astype(F32)
    pulls = high + pltpu.roll(pulls - high, 3, 0)
    f_rows = jnp.concatenate(
        [pulls * block_of[pl.ds(i, 1), :].astype(F32) for i in range(blocks)], axis=0
    ).astype(BF16)
    f_all[...] = mm_nt(f_rows, slot_of[...])
    first = (atoms // sends) * unit
    span_y, span_x = 9 * unit, 3 * unit
    f_y = [
        send(f_all.at[pl.ds(first + part * span_y, span_y)], f_recv_y.at[slot], "gy", by)
        for slot, part, by in ((0, 0, -1), (1, 2, 1))
    ]
    total = mm_nt(pulls.astype(BF16), onehot_c[...])
    for j in range(atoms // sends):
        block = f_all[pl.ds(j * unit, unit), :]
        total = total - (block if j == 0 else pltpu.roll(block, j * sends, 1))
    for copy in f_y:
        copy.wait_recv()
    lines = f_all[pl.ds(first + span_y, span_y), :] + f_recv_y[0] + f_recv_y[1]
    f_x = []
    for slot, part, by in ((0, 0, -1), (1, 2, 1)):
        f_send_x[slot] = lines[part * span_x : (part + 1) * span_x]
        f_x.append(send(f_send_x.at[slot], f_recv_x.at[slot], "gx", by))
    for copy in f_x:
        copy.wait_recv()
    lines = lines[span_x : 2 * span_x] + f_recv_x[0] + f_recv_x[1]
    f_z = []
    for slot, part, by in ((0, 0, -1), (1, 2, 1)):
        f_send_z[slot] = lines[part * unit : (part + 1) * unit]
        f_z.append(send(f_send_z.at[slot], f_recv_z.at[slot], "gz", by))
    for copy in f_z:
        copy.wait_recv()
    lines = lines[unit : 2 * unit] + f_recv_z[0] + f_recv_z[1]
    total = total - joined(mm(split(lines), lend_wide))
    for row in range(3):
        forces[row] = total[row : row + 1] + total[row + 3 : row + 4]
    for copy in started:
        copy.wait_send()


def per_device(
    species, atom_count, send_list, edge_count, edge_center, edge_neighbour, edge_vectors,
    embed, w_src, w_rad0, w_rad1, w_inv, w_out, w_gate, w_energy,
):
    atoms = species.shape[-1]
    edges = edge_center.shape[-1]
    sends = send_list.shape[-1]
    width = w_out.shape[1]
    chan = w_gate.shape[2]
    hid = w_rad0.shape[2]
    cols = width + 8 * chan
    ghosts = 27 * sends
    unit = 8
    vmem = pl.BlockSpec(memory_space=pltpu.VMEM)
    smem = pl.BlockSpec(memory_space=pltpu.SMEM)
    hbm = pl.BlockSpec(memory_space=pl.ANY)
    copies = 26 + 26 + 14 + 6
    operands = (
        species.reshape(1, atoms), send_list.reshape(1, sends), edge_vectors.reshape(3, 1, edges),
        edge_neighbour.reshape(1, edges), edge_center.reshape(1, edges),
        embed, jnp.swapaxes(w_src, 1, 2), w_rad0, w_rad1, w_inv, w_out, jnp.swapaxes(w_gate, 1, 2),
        w_energy.reshape(1, width),
    )
    energies, forces = pl.pallas_call(
        body,
        out_shape=(
            jax.ShapeDtypeStruct((1, atoms), F32),
            jax.ShapeDtypeStruct((3, 1, atoms), F32),
        ),
        in_specs=[smem, smem] + [hbm] * len(operands),
        out_specs=(vmem, vmem),
        scratch_shapes=[pltpu.VMEM(operand.shape, operand.dtype) for operand in operands] + [
            pltpu.VMEM((atoms + ghosts, edges), BF16),
            pltpu.VMEM((atoms, edges), BF16),
            pltpu.VMEM((32, edges), BF16),
            pltpu.VMEM((atoms, edges), BF16),
            pltpu.VMEM((27 * unit, atoms), F32),
            pltpu.VMEM((ghosts, cols), BF16),
            pltpu.VMEM((cols, atoms + ghosts), BF16),
            pltpu.VMEM((cols, edges), BF16),
            pltpu.VMEM((cols, edges), BF16),
            pltpu.VMEM((8, edges), F32),
            pltpu.VMEM((8, edges), F32),
            pltpu.VMEM((8, edges), F32),
            pltpu.VMEM((16, edges), F32),
            pltpu.VMEM((2 * hid, edges), F32),
            pltpu.VMEM((width + chan, edges), F32),
            pltpu.VMEM((width, edges), F32),
            pltpu.VMEM((width + chan, edges), F32),
            pltpu.VMEM((cols, atoms), F32),
            pltpu.VMEM((width, atoms), F32),
            pltpu.VMEM((8, edges), F32),
            pltpu.VMEM((1, edges), F32),
            pltpu.VMEM((8, edges), F32),
            pltpu.VMEM((2, 9 * sends, cols), BF16),
            pltpu.VMEM((2, 9 * sends, cols), BF16),
            pltpu.VMEM((2, 3 * sends, cols), BF16),
            pltpu.VMEM((2, 3 * sends, cols), BF16),
            pltpu.VMEM((2, sends, cols), BF16),
            pltpu.VMEM((2, sends, cols), BF16),
            pltpu.VMEM(((atoms // sends + 27) * unit, 128), F32),
            pltpu.VMEM((2, 9 * unit, 128), F32),
            pltpu.VMEM((2, 3 * unit, 128), F32),
            pltpu.VMEM((2, 3 * unit, 128), F32),
            pltpu.VMEM((2, unit, 128), F32),
            pltpu.VMEM((2, unit, 128), F32),
            pltpu.SemaphoreType.DMA((copies,)),
            pltpu.SemaphoreType.DMA((copies,)),
            pltpu.SemaphoreType.DMA((len(operands),)),
        ],
        compiler_params=pltpu.CompilerParams(
            collective_id=0, has_side_effects=True, vmem_limit_bytes=56 * 1024 * 1024
        ),
    )(atom_count, edge_count, *operands)
    return energies.reshape(species.shape), forces.reshape(edge_vectors.shape[:3] + (3, atoms))


def solution(mesh):
    shard = P("gx", "gy", "gz", None)
    count = P("gx", "gy", "gz")
    wide = P("gx", "gy", "gz", None, None)
    return jax.shard_map(
        per_device,
        mesh=mesh,
        in_specs=(shard, count, shard, count, shard, shard, wide) + (P(),) * 8,
        out_specs=(shard, wide),
        check_vma=False,
    )
```

time: 96.9 us -> 73.8 us (0.76)
  Pallas kernels: 91 us -> 69.1 us
  local copies, waits for them, and re-layouts: 3.52 us -> 1.69 us
    pallas_call x1, Pallas kernels: 91 us -> 69.1 us  [per_device(): pl.pallas_call(body, out_shape=(jax.ShapeDtypeStruct((1, atoms), F32), ja...]
    unnamed x27 -> x6, local copies, waits for them, and re-layouts: 3.52 us -> 1.69 us
where the time goes in v1:
time: 73.8 us; the launch traced here: 72.7 us
  Pallas kernels  69.1 us (94%)
  between operations  1.95 us (3%)
  local copies, waits for them, and re-layouts  1.69 us (2%)
    pallas_call x1, Pallas kernels, per_device(): pl.pallas_call(body, out_shape=(jax.ShapeDtypeStruct((1, atoms), F32), ja...  69.1 us
    unnamed x6, local copies, waits for them, and re-layouts  1.69 us

profile of v1, /device:TPU:1, one launch (start us, length us, event | category | flops | bytes accessed | tf_op | source)
XLA Modules:
  0.0 72.7 jit_solution(11344209172298174378)
XLA Ops:
  1.9 69.1 %shard_map.158 = (f32[1,128]{1,0:T(1,128)}, f32[3,1,128]{2,1,0:T(1,128)}) custom-call(s32[1,1,1]{2,1,0:T(1,128)S(6)} %copy.20.atom_count, s32[1,1,1]{2,1,0:T(1,128)S(6)} %copy.21.edge_count, s32[1,128]{1,0:T(1,128)} %bitcast.18, s32[1,32]{1,0:T(1,128)} %bitcast.19, f32[3,1,2560]{2,1,0:T(1,128)} %bitcast.14, s32[1,2560]{1,0:T(1,128)} %bitcast.15, ...), custom_call_target="tpu_custom_call" | custom-call | tf_op jit(solution)/shard_map/pallas_call | solution.py:496
  71.0 0.0 copy-start.1
  71.0 0.0 copy-start
  71.0 0.6 copy-done.1
  71.7 0.5 copy.22
  72.2 0.0 copy-done
  72.2 0.6 copy.23
Async XLA Ops:
  71.0 0.6 copy-start.1
  71.0 1.1 %copy-start = (f32[3,1,128]{2,1,0:T(1,128)S(1)}, f32[3,1,128]{2,1,0:T(1,128)}, u32[]{:S(2)}) copy-start(f32[3,1,128]{2,1,0:T(1,128)} %get-tuple-element.5) | copy-start | bytes 4612

commit v2 on v1

--- a/solution.py
+++ b/solution.py
@@ -10,7 +10,19 @@
 
 RADIAL = 8
 CUTOFF = 5.0
-TILE = 1280
+PLANE = ((1, 0), (1, 1), (1, 2), (0, 1), (2, 1), (0, 0), (0, 2), (2, 0), (2, 2))
+REST = 5
+
+
+def position(b, a, c):
+    index = PLANE.index((c, a))
+    if b == 1:
+        return index
+    if index < REST:
+        return 9 + (b // 2) * REST + index
+    return 9 + 2 * REST + (b // 2) * (9 - REST) + index - REST
+
+
 MESH = pl.DeviceIdType.MESH
 BF16 = jnp.bfloat16
 F32 = jnp.float32
@@ -65,8 +77,8 @@
 ):
     args, (energies, forces), held = refs[:13], refs[13:15], refs[15:28]
     (
-        onehot, onehot_c, block_of, slot_of, kinds, halo, table, picked, dmsg,
-        geo, harm, dbas, basis, slope, rad1, rad2, proj1, agg, agg2, grad_y, grad_d, pull,
+        onehot, onehot_c, block_of, slot_of, kinds, halo, table, last_table, picked, dmsg,
+        geo, harm, dbas, basis, slope, rad1, rad2, proj1, src2, gate_w, inv_t, out_t, kind_proj, start, readout, f_rows, agg, agg2, grad_y, grad_d, pull,
         back_send_y, back_recv_y, back_send_x, back_recv_x, back_send_z, back_recv_z,
         f_all, f_recv_y, f_send_x, f_recv_x, f_send_z, f_recv_z,
         send_sems, recv_sems, arg_sems,
@@ -80,10 +92,10 @@
     sends = send_list.shape[1]
     width = w_out.shape[1]
     chan = w_gate.shape[1]
-    rows_x = 3 * sends
     rows_y = 9 * sends
-    ghosts = 27 * sends
-    tiles = edges // TILE
+    rest = REST * sends
+    corner = 9 * sends - rest
+    early = atoms + 27 * sends - 2 * corner
     unit = 8
     blocks = atoms // sends + 27
 
@@ -119,7 +131,7 @@
 
     def spread(ref, size, between):
         def at(b, a, c):
-            return ref.at[pl.ds(((b * 3 + a) * 3 + c) * size, size)]
+            return ref.at[pl.ds(position(b, a, c) * size, size)]
 
         def along(axis, b, a, c):
             sides = {"gz": ((b, a, 0), (b, a, 2)), "gx": ((b, 0, c), (b, 2, c)), "gy": ((0, a, c), (2, a, c))}
@@ -140,10 +152,12 @@
         in_y += along("gy", 1, 1, 0) + along("gy", 1, 1, 2)
         between[1]()
         arrived(in_x)
+        last = []
         for c in (0, 2):
-            in_y += along("gy", 1, 0, c) + along("gy", 1, 2, c)
+            last += along("gy", 1, 0, c) + along("gy", 1, 2, c)
+        arrived(in_y)
         between[2]()
-        arrived(in_y)
+        arrived(last)
 
     loads[0].wait()
     loads[1].wait()
@@ -155,8 +169,9 @@
     lend_wide = mm_nt(eye(128, sends), lend_t).astype(BF16)
     lend = lend_wide[:sends]
     species_rows = jnp.broadcast_to(species[...].astype(F32), (unit, atoms))
-    kinds[pl.ds(13 * unit, unit), :] = mm_nt(species_rows.astype(BF16), lend_wide)
+    kinds[pl.ds(position(1, 1, 1) * unit, unit), :] = mm_nt(species_rows.astype(BF16), lend_wide)
     pl.semaphore_wait(barrier, 6)
+
 
     def geometry():
         for load in loads[2:5]:
@@ -188,26 +203,36 @@
             dbas[pl.ds(k - 1, 1), :] = (k * math.pi / CUTOFF) * cos_k * scale + sin_k * dscale
             sin_k, cos_k = sin_k * cosine + cos_k * sine, cos_k * cosine - sin_k * sine
 
-        near = neighbour[...]
-        ghost = near - atoms
-        part_a = jnp.where(ghost >= rows_y, 1, 0) + jnp.where(ghost >= 2 * rows_y, 1, 0)
-        ghost = ghost - rows_y * part_a
-        part_b = jnp.where(ghost >= rows_x, 1, 0) + jnp.where(ghost >= 2 * rows_x, 1, 0)
-        ghost = ghost - rows_x * part_b + rows_x * part_a + rows_y * part_b + atoms
-        place = jnp.where(live, jnp.where(near < atoms, near, ghost), -1)
+        place = jnp.where(live, neighbour[...], -1)
         middle = jnp.where(live, center[...], -1)
         block = lax.shift_right_arithmetic(place, sends.bit_length() - 1)
         slot = lax.bitwise_and(place, sends - 1)
-        rows = lax.broadcasted_iota(jnp.int32, (32, edges), 0)
-        block_of[...] = jnp.where(rows == block, 1.0, 0.0).astype(BF16)
+        order = {position(b, a, c): (a * 3 + b) * 3 + c for a in range(3) for b in range(3) for c in range(3)}
+        rows = lax.broadcasted_iota(jnp.int32, (32, 1), 0)
+        block_ids = rows
+        for i in range(27):
+            block_ids = jnp.where(rows == atoms // sends + i, atoms // sends + order[i], block_ids)
+        block_of[...] = jnp.where(block_ids == block, 1.0, 0.0).astype(BF16)
         rows = lax.broadcasted_iota(jnp.int32, (atoms, edges), 0)
         slot_of[...] = jnp.where(rows == slot, 1.0, 0.0).astype(BF16)
         onehot_c[...] = jnp.where(rows == middle, 1.0, 0.0).astype(BF16)
-        rows = lax.broadcasted_iota(jnp.int32, onehot.shape, 0)
-        onehot[...] = jnp.where(rows == place, 1.0, 0.0).astype(BF16)
-
-    def cut(i):
-        return pl.ds(pl.multiple_of(i * TILE, TILE), TILE)
+        onehot[pl.ds(0, atoms), :] = jnp.where(rows == place, 1.0, 0.0).astype(BF16)
+        rows = lax.broadcasted_iota(jnp.int32, (sends, edges), 0)
+        for i in range(27):
+            onehot[pl.ds(atoms + i * sends, sends), :] = jnp.where(
+                rows == place - (atoms + order[i] * sends), 1.0, 0.0
+            ).astype(BF16)
+
+    def sweep(tile, work):
+        if tile < 0:
+            for i in range(edges // -tile):
+                work(pl.ds(i * -tile, -tile))
+        elif tile == edges:
+            work(pl.ds(0, edges))
+        else:
+            lax.fori_loop(
+                0, edges // tile, lambda i, carry: (work(pl.ds(pl.multiple_of(i * tile, tile), tile)), carry)[1], 0
+            )
 
     def radial():
         for load in loads[5:]:
@@ -226,121 +251,117 @@
         rad1_t1 = turned(w_rad1[0][:, : width + chan])
         rad1_t2 = turned(w_rad1[1][:, :width])
 
-        def prepare(i, carry):
-            span = cut(i)
+        def prepare(span):
             pre = mm(rad0_t, basis[:, span].astype(BF16))
             sig = jax.nn.sigmoid(pre)
             slope[:, span] = sig * (1.0 + pre * (1.0 - sig))
             hidden = (pre * sig).astype(BF16)
             rad1[:, span] = mm(rad1_t1, hidden[:hid])
             rad2[:, span] = mm(rad1_t2, hidden[hid:])
-            return carry
-
-        lax.fori_loop(0, tiles, prepare, 0)
+
+        sweep(edges, prepare)
+
+        src2[...] = turned(w_src[1][:width])
+        gate_w[...] = turned(w_gate[0])
+        inv_t[...] = turned(w_inv[1])
+        for layer in range(2):
+            out_t[layer] = turned(w_out[layer])
+        embed_rows = jnp.concatenate([embed[...], jnp.zeros((16 - embed.shape[0], width), F32)], axis=0)
+        embed_t = turned(embed_rows.astype(BF16))
+        kind_proj[...] = mm(w_src[0], embed_t).astype(BF16)
+        start[...] = mm(embed_t, kind_t[:16, :])
+        readout[...] = jnp.broadcast_to(w_energy[...], (width, width)).T
 
     root = math.sqrt(3.0)
     hid = w_rad0.shape[2]
     spread(kinds, unit, (geometry, radial, lambda: None))
-    src1_t = w_src[0]
-    src2_t = w_src[1]
-    src2 = turned(src2_t[:width])
-    inv_t = turned(w_inv[1])
-    out1_t = turned(w_out[0])
-    out2_t = turned(w_out[1])
-    gate_t = w_gate[0]
-    embed_rows = jnp.concatenate([embed[...], jnp.zeros((16 - embed.shape[0], width), F32)], axis=0)
-    embed_t = turned(embed_rows.astype(BF16))
-    kind_proj = mm(src1_t, embed_t).astype(BF16)
-    start = mm(embed_t, kind_t[:16, :])
-
     number = species_rows[:1]
     kind_rows = [number] + [pltpu.roll(number, atoms - j * sends, 1) for j in range(1, atoms // sends)]
     kind_rows += [kinds[pl.ds(i * unit, 1), :] for i in range(27)]
     kind_rows += [jnp.zeros((1, atoms), F32)] * (32 - blocks)
     kind_table = mm_nt(eye(sends, atoms), jnp.concatenate(kind_rows, axis=0).astype(BF16)).astype(BF16)
-    agg[...] = jnp.zeros_like(agg)
-
-    def layer_one(i, carry):
-        span = cut(i)
+
+    def layer_one(span):
         kind = sum_rows(mm(kind_table, block_of[:, span]) * slot_of[pl.ds(0, sends), span].astype(F32))
-        kind_ids = lax.broadcasted_iota(jnp.int32, (16, TILE), 0).astype(F32)
-        proj = mm(kind_proj, jnp.where(kind_ids == kind, 1.0, 0.0).astype(BF16))
+        kind_ids = lax.broadcasted_iota(jnp.int32, (16, kind.shape[1]), 0).astype(F32)
+        proj = mm(kind_proj[...], jnp.where(kind_ids == kind, 1.0, 0.0).astype(BF16))
         proj1[:, span] = proj
         lead_s = proj[:width] * rad1[pl.ds(0, width), span]
         lead_t = proj[width:] * rad1[pl.ds(width, chan), span]
         parts = [lead_s.astype(BF16)]
         for m in range(8):
             parts.append((lead_t * harm[pl.ds(m, 1), span]).astype(BF16))
-        agg[...] += mm_nt(jnp.concatenate(parts, axis=0), onehot_c[:, span])
-        return carry
-
-    lax.fori_loop(0, tiles, layer_one, 0)
+        agg[...] = mm_nt(jnp.concatenate(parts, axis=0), onehot_c[:, span])
+
+    sweep(edges, layer_one)
     gathered = 0.25 * agg[...]
     gathered_t = gathered[width:]
     rounded = gathered[:width].astype(BF16)
-    pre1 = mm(out1_t, rounded)
+    pre1 = mm(out_t[0], rounded)
     sig1 = jax.nn.sigmoid(pre1)
-    gate = jax.nn.sigmoid(mm(gate_t, rounded))
-    scalars = (start + pre1 * sig1).astype(BF16)
+    gate = jax.nn.sigmoid(mm(w_gate[0], rounded))
+    scalars = (start[...] + pre1 * sig1).astype(BF16)
     gates = jnp.concatenate([gate] * 8, axis=0)
     tensors = (gathered_t * gates).astype(BF16)
-    proj2 = mm(src2_t, scalars).astype(BF16)
+    proj2 = mm(w_src[1], scalars).astype(BF16)
     local = jnp.concatenate([proj2[:width], tensors], axis=0)
-    halo[pl.ds(13 * sends, sends), :] = mm_nt(lend, local).astype(BF16)
+    halo[pl.ds(position(1, 1, 1) * sends, sends), :] = mm_nt(lend, local).astype(BF16)
     table[:, pl.ds(0, atoms)] = local
     nothing = lambda: None
-    spread(halo, sends, (nothing, nothing, nothing))
-    table[:, pl.ds(atoms, ghosts)] = halo[...].T
-    agg2[...] = jnp.zeros_like(agg2)
-
-    def layer_two(i, carry):
-        span = cut(i)
-        rows = mm(table[...], onehot[pl.ds(0, atoms + ghosts), span])
+
+    def lookup(span):
+        picked[:, span] = mm(table[...], onehot[pl.ds(0, early), span]).astype(BF16)
+
+    def early_rows():
+        table[:, pl.ds(atoms, early - atoms)] = halo[pl.ds(0, early - atoms), :].T
+        sweep(edges, lookup)
+
+    spread(halo, sends, (nothing, nothing, early_rows))
+    last_table[...] = halo[pl.ds(early - atoms, 2 * corner), :].T
+
+    def layer_two(span):
+        rows = picked[:, span].astype(F32) + mm(last_table[...], onehot[pl.ds(early, 2 * corner), span])
         picked[:, span] = rows.astype(BF16)
-        inner = jnp.zeros((chan, TILE), F32)
+        inner = jnp.zeros((chan, span.size), F32)
         for m in range(8):
             inner += rows[width + m * chan : width + (m + 1) * chan] * harm[pl.ds(m, 1), span]
-        message = rows[:width] * rad2[:, span] + mm(inv_t, inner.astype(BF16))
-        agg2[...] += mm_nt(message.astype(BF16), onehot_c[:, span])
-        return carry
-
-    lax.fori_loop(0, tiles, layer_two, 0)
+        message = rows[:width] * rad2[:, span] + mm(inv_t[...], inner.astype(BF16))
+        agg2[...] = mm_nt(message.astype(BF16), onehot_c[:, span])
+
+    sweep(edges, layer_two)
     rounded = (0.25 * agg2[...]).astype(BF16)
-    pre2 = mm(out2_t, rounded)
+    pre2 = mm(out_t[1], rounded)
     sig2 = jax.nn.sigmoid(pre2)
-    readout = jnp.broadcast_to(w_energy[...], (width, width)).T[:, :1]
     mask = jnp.where(
         lax.broadcasted_iota(jnp.int32, (1, atoms), 1) < atom_count[0, 0, 0], 1.0, 0.0
     )
-    energies[...] = mask * sum_rows((scalars.astype(F32) + pre2 * sig2) * readout)
-
-    d_new = readout * mask
+    energies[...] = mask * sum_rows((scalars.astype(F32) + pre2 * sig2) * readout[...])
+
+    d_new = readout[...] * mask
     d_pre = (d_new * sig2 * (1.0 + pre2 * (1.0 - sig2))).astype(BF16)
     d_agg = (0.25 * mm(w_out[1], d_pre).astype(BF16).astype(F32)).astype(BF16)
 
-    def back_two(i, carry):
-        span = cut(i)
+    def back_two(span):
         d_msg = mm(d_agg, onehot_c[:, span])
         dmsg[pl.ds(0, width), span] = (d_msg * rad2[:, span]).astype(BF16)
         d_inv = mm(w_inv[1], d_msg.astype(BF16))
         for m in range(8):
             dmsg[pl.ds(width + m * chan, chan), span] = (d_inv * harm[pl.ds(m, 1), span]).astype(BF16)
-        return carry
-
-    lax.fori_loop(0, tiles, back_two, 0)
+
+    sweep(edges, back_two)
     back_y = {}
-    for slot, part, by in ((0, 0, -1), (1, 2, 1)):
-        back_send_y[slot] = mm_nt(
-            onehot[pl.ds(atoms + part * rows_y, rows_y), :], dmsg[...]
-        ).astype(BF16)
-        for a in (0, 2, 1):
-            rows = pl.ds(a * rows_x, rows_x)
-            back_y[slot, a] = send(back_send_y.at[slot, rows], back_recv_y.at[slot, rows], "gy", by)
-    back = mm_nt(onehot[pl.ds(atoms + rows_y, rows_y), :], dmsg[...])
+    parity = lax.rem(lax.axis_index("gy"), 2)
+    for slot, by in ((0, 2 * parity - 1), (1, 1 - 2 * parity)):
+        side = (by + 1) // 2
+        for piece, first, size, count in ((1, 9 * sends + 2 * rest, corner, corner), (0, 9 * sends, rest, rest)):
+            rows = pl.ds(rest if piece else 0, size)
+            start_row = pl.multiple_of(atoms + first + side * count, sends)
+            back_send_y[slot, rows] = mm_nt(onehot[pl.ds(start_row, size), :], dmsg[...]).astype(BF16)
+            back_y[slot, piece] = send(back_send_y.at[slot, rows], back_recv_y.at[slot, rows], "gy", by)
+    back = mm_nt(onehot[pl.ds(atoms, rows_y), :], dmsg[...])
     d_local = mm_nt(dmsg[...], onehot[pl.ds(0, atoms), :])
 
-    def edge_two(i, carry):
-        span = cut(i)
+    def edge_two(span):
         d_msg = mm(d_agg, onehot_c[:, span])
         d_inv = mm(w_inv[1], d_msg.astype(BF16))
         for m in range(8):
@@ -351,34 +372,35 @@
         d_hid = mm(w_rad1[1][:, :width], d_rad) * slope[pl.ds(hid, hid), span]
         d_bas = mm(w_rad0[1], d_hid.astype(BF16))
         grad_d[:, span] = sum_rows(d_bas * dbas[:, span])
-        return carry
-
-    lax.fori_loop(0, tiles, edge_two, 0)
-
-    def merged(a):
-        rows = pl.ds(a * rows_x, rows_x)
+
+    sweep(edges, edge_two)
+
+    def merged(piece):
+        rows = pl.ds(rest if piece else 0, corner if piece else rest)
         for slot in range(2):
-            back_y[slot, a].wait_recv()
+            back_y[slot, piece].wait_recv()
         return (
-            back[a * rows_x : (a + 1) * rows_x] + back_recv_y[0, rows].astype(F32) + back_recv_y[1, rows].astype(F32)
+            back[rows.start : rows.start + rows.size]
+            + back_recv_y[0, rows].astype(F32) + back_recv_y[1, rows].astype(F32)
         )
 
     back_x = {}
-    for slot, part, by in ((0, 0, -1), (1, 2, 1)):
-        back_send_x[slot] = merged(part).astype(BF16)
-        for c in (0, 2, 1):
-            rows = pl.ds(c * sends, sends)
-            back_x[slot, c] = send(back_send_x.at[slot, rows], back_recv_x.at[slot, rows], "gx", by)
-    middle_rows = merged(1)
+    plane = {}
+    for piece in (1, 0):
+        sums = merged(piece)
+        for i, (c, a) in enumerate(PLANE[REST:] if piece else PLANE[:REST]):
+            plane[c, a] = sums[i * sends : (i + 1) * sends]
+        for c in (0, 2) if piece else (1,):
+            for slot, part, by in ((0, 0, -1), (1, 2, 1)):
+                rows = pl.ds(c * sends, sends)
+                back_send_x[slot, rows] = plane[c, part].astype(BF16)
+                back_x[slot, c] = send(back_send_x.at[slot, rows], back_recv_x.at[slot, rows], "gx", by)
 
     def gathered_x(c):
         rows = pl.ds(c * sends, sends)
         for slot in range(2):
             back_x[slot, c].wait_recv()
-        return (
-            middle_rows[c * sends : (c + 1) * sends]
-            + back_recv_x[0, rows].astype(F32) + back_recv_x[1, rows].astype(F32)
-        )
+        return plane[c, 1] + back_recv_x[0, rows].astype(F32) + back_recv_x[1, rows].astype(F32)
 
     back_z = []
     for slot, part, by in ((0, 0, -1), (1, 2, 1)):
@@ -390,7 +412,7 @@
     back = back + back_recv_z[0].astype(F32) + back_recv_z[1].astype(F32)
     owned = d_local + mm(back.T.astype(BF16), lend)
 
-    d_scalars = (d_new + mm(src2, owned[:width].astype(BF16))).astype(BF16).astype(F32)
+    d_scalars = (d_new + mm(src2[...], owned[:width].astype(BF16))).astype(BF16).astype(F32)
     d_tensors = owned[width:].astype(BF16).astype(F32)
     d_pre = (d_scalars * sig1 * (1.0 + pre1 * (1.0 - sig1))).astype(BF16)
     product = d_tensors * gathered_t
@@ -398,15 +420,14 @@
     for m in range(8):
         d_gate += product[m * chan : (m + 1) * chan]
     d_gate = (d_gate * gate * (1.0 - gate)).astype(BF16)
-    d_scalar_agg = (mm(w_out[0], d_pre) + mm(turned(gate_t), d_gate)).astype(BF16).astype(F32)
+    d_scalar_agg = (mm(w_out[0], d_pre) + mm(gate_w[...], d_gate)).astype(BF16).astype(F32)
     d_agg1 = (0.25 * jnp.concatenate([d_scalar_agg, d_tensors * gates], axis=0)).astype(BF16)
 
-    def edge_one(i, carry):
-        span = cut(i)
+    def edge_one(span):
         d_msg = mm(d_agg1, onehot_c[:, span])
         proj = proj1[:, span]
         lead_t = proj[width:] * rad1[pl.ds(width, chan), span]
-        inner = jnp.zeros((chan, TILE), F32)
+        inner = jnp.zeros((chan, span.size), F32)
         gy = []
         for m in range(8):
             d_part = d_msg[width + m * chan : width + (m + 1) * chan]
@@ -424,38 +445,42 @@
         pull[pl.ds(0, 1), span] = geo[3:4, span] * gux + ax * radial
         pull[pl.ds(1, 1), span] = geo[3:4, span] * guy + ay * radial
         pull[pl.ds(2, 1), span] = geo[3:4, span] * guz + az * radial
-        return carry
 
     pull[...] = jnp.zeros_like(pull)
-    lax.fori_loop(0, tiles, edge_one, 0)
+    sweep(edges, edge_one)
 
     pulls = pull[...]
     high = pulls.astype(BF16).astype(F32)
     pulls = high + pltpu.roll(pulls - high, 3, 0)
-    f_rows = jnp.concatenate(
-        [pulls * block_of[pl.ds(i, 1), :].astype(F32) for i in range(blocks)], axis=0
-    ).astype(BF16)
-    f_all[...] = mm_nt(f_rows, slot_of[...])
+    for i in range(0, 32, 2):
+        f_rows[pl.ds(i * unit, 2 * unit), :] = jnp.concatenate(
+            [pulls * block_of[pl.ds(j, 1), :].astype(F32) for j in (i, i + 1)], axis=0
+        ).astype(BF16)
+    f_all[...] = mm_nt(f_rows[...], slot_of[...])
     first = (atoms // sends) * unit
-    span_y, span_x = 9 * unit, 3 * unit
-    f_y = [
-        send(f_all.at[pl.ds(first + part * span_y, span_y)], f_recv_y.at[slot], "gy", by)
-        for slot, part, by in ((0, 0, -1), (1, 2, 1))
-    ]
+    f_y = []
+    for slot, part, by in ((0, 0, -1), (1, 2, 1)):
+        for index, count in ((REST, 9 - REST), (0, REST)):
+            c, a = PLANE[index]
+            f_y.append(send(
+                f_all.at[pl.ds(first + position(part, a, c) * unit, count * unit)],
+                f_recv_y.at[slot, pl.ds(index * unit, count * unit)], "gy", by,
+            ))
     total = mm_nt(pulls.astype(BF16), onehot_c[...])
     for j in range(atoms // sends):
         block = f_all[pl.ds(j * unit, unit), :]
         total = total - (block if j == 0 else pltpu.roll(block, j * sends, 1))
     for copy in f_y:
         copy.wait_recv()
-    lines = f_all[pl.ds(first + span_y, span_y), :] + f_recv_y[0] + f_recv_y[1]
+    lines = f_all[pl.ds(first, 9 * unit), :] + f_recv_y[0] + f_recv_y[1]
+    cells = {cell: lines[i * unit : (i + 1) * unit] for i, cell in enumerate(PLANE)}
     f_x = []
     for slot, part, by in ((0, 0, -1), (1, 2, 1)):
-        f_send_x[slot] = lines[part * span_x : (part + 1) * span_x]
+        f_send_x[slot] = jnp.concatenate([cells[c, part] for c in range(3)], axis=0)
         f_x.append(send(f_send_x.at[slot], f_recv_x.at[slot], "gx", by))
     for copy in f_x:
         copy.wait_recv()
-    lines = lines[span_x : 2 * span_x] + f_recv_x[0] + f_recv_x[1]
+    lines = jnp.concatenate([cells[c, 1] for c in range(3)], axis=0) + f_recv_x[0] + f_recv_x[1]
     f_z = []
     for slot, part, by in ((0, 0, -1), (1, 2, 1)):
         f_send_z[slot] = lines[part * unit : (part + 1) * unit]
@@ -483,10 +508,11 @@
     cols = width + 8 * chan
     ghosts = 27 * sends
     unit = 8
+    early = atoms + (9 + 2 * REST) * sends
     vmem = pl.BlockSpec(memory_space=pltpu.VMEM)
     smem = pl.BlockSpec(memory_space=pltpu.SMEM)
-    hbm = pl.BlockSpec(memory_space=pl.ANY)
-    copies = 26 + 26 + 14 + 6
+    hbm = pl.BlockSpec(memory_space=pltpu.HBM)
+    copies = 26 + 26 + 12 + 8
     operands = (
         species.reshape(1, atoms), send_list.reshape(1, sends), edge_vectors.reshape(3, 1, edges),
         edge_neighbour.reshape(1, edges), edge_center.reshape(1, edges),
@@ -508,7 +534,8 @@
             pltpu.VMEM((atoms, edges), BF16),
             pltpu.VMEM((27 * unit, atoms), F32),
             pltpu.VMEM((ghosts, cols), BF16),
-            pltpu.VMEM((cols, atoms + ghosts), BF16),
+            pltpu.VMEM((cols, early), BF16),
+            pltpu.VMEM((cols, ghosts + atoms - early), BF16),
             pltpu.VMEM((cols, edges), BF16),
             pltpu.VMEM((cols, edges), BF16),
             pltpu.VMEM((8, edges), F32),
@@ -519,6 +546,14 @@
             pltpu.VMEM((width + chan, edges), F32),
             pltpu.VMEM((width, edges), F32),
             pltpu.VMEM((width + chan, edges), F32),
+            pltpu.VMEM((width, width), BF16),
+            pltpu.VMEM((width, chan), BF16),
+            pltpu.VMEM((width, chan), BF16),
+            pltpu.VMEM((2, width, width), BF16),
+            pltpu.VMEM((width + chan, 16), BF16),
+            pltpu.VMEM((width, atoms), F32),
+            pltpu.VMEM((width, width), F32),
+            pltpu.VMEM((32 * unit, edges), BF16),
             pltpu.VMEM((cols, atoms), F32),
             pltpu.VMEM((width, atoms), F32),
             pltpu.VMEM((8, edges), F32),
@@ -530,7 +565,7 @@
             pltpu.VMEM((2, 3 * sends, cols), BF16),
             pltpu.VMEM((2, sends, cols), BF16),
             pltpu.VMEM((2, sends, cols), BF16),
-            pltpu.VMEM(((atoms // sends + 27) * unit, 128), F32),
+            pltpu.VMEM((32 * unit, 128), F32),
             pltpu.VMEM((2, 9 * unit, 128), F32),
             pltpu.VMEM((2, 3 * unit, 128), F32),
             pltpu.VMEM((2, 3 * unit, 128), F32),

time: 73.8 us -> 70.7 us (0.958)
  Pallas kernels: 69.1 us -> 66.4 us
    pallas_call x1, Pallas kernels: 69.1 us -> 66.4 us  [per_device(): pl.pallas_call(body, out_shape=(jax.ShapeDtypeStruct((1, atoms), F32), ja...]
where the time goes in v2:
time: 70.7 us; the launch traced here: 70.1 us
  Pallas kernels  66.4 us (94%)
  between operations  1.95 us (3%)
  local copies, waits for them, and re-layouts  1.69 us (2%)
    pallas_call x1, Pallas kernels, per_device(): pl.pallas_call(body, out_shape=(jax.ShapeDtypeStruct((1, atoms), F32), ja...  66.4 us
    unnamed x6, local copies, waits for them, and re-layouts  1.69 us

profile of v2, /device:TPU:1, one launch (start us, length us, event | category | flops | bytes accessed | tf_op | source)
XLA Modules:
  0.0 70.1 jit_solution(11109253669816060795)
XLA Ops:
  1.9 66.4 %shard_map.158 = (f32[1,128]{1,0:T(1,128)}, f32[3,1,128]{2,1,0:T(1,128)}) custom-call(s32[1,1,1]{2,1,0:T(1,128)S(6)} %copy.20.atom_count, s32[1,1,1]{2,1,0:T(1,128)S(6)} %copy.21.edge_count, s32[1,128]{1,0:T(1,128)} %bitcast.18, s32[1,32]{1,0:T(1,128)} %bitcast.19, f32[3,1,2560]{2,1,0:T(1,128)} %bitcast.14, s32[1,2560]{1,0:T(1,128)} %bitcast.15, ...), custom_call_target="tpu_custom_call" | custom-call | tf_op jit(solution)/shard_map/pallas_call | solution.py:522
  68.4 0.0 copy-start.1
  68.4 0.0 copy-start
  68.4 0.6 copy-done.1
  69.0 0.5 copy.22
  69.5 0.0 copy-done
  69.5 0.6 copy.23
Async XLA Ops:
  68.4 0.6 copy-start.1
  68.4 1.1 %copy-start = (f32[3,1,128]{2,1,0:T(1,128)S(1)}, f32[3,1,128]{2,1,0:T(1,128)}, u32[]{:S(2)}) copy-start(f32[3,1,128]{2,1,0:T(1,128)} %get-tuple-element.5) | copy-start | bytes 4612

commit v3 on v2

--- a/solution.py
+++ b/solution.py
@@ -12,11 +12,12 @@
 CUTOFF = 5.0
 PLANE = ((1, 0), (1, 1), (1, 2), (0, 1), (2, 1), (0, 0), (0, 2), (2, 0), (2, 2))
 REST = 5
+OTHER, OWN, MATE = 0, 1, 2
 
 
 def position(b, a, c):
     index = PLANE.index((c, a))
-    if b == 1:
+    if b == OWN:
         return index
     if index < REST:
         return 9 + (b // 2) * REST + index
@@ -79,8 +80,8 @@
     (
         onehot, onehot_c, block_of, slot_of, kinds, halo, table, last_table, picked, dmsg,
         geo, harm, dbas, basis, slope, rad1, rad2, proj1, src2, gate_w, inv_t, out_t, kind_proj, start, readout, f_rows, agg, agg2, grad_y, grad_d, pull,
-        back_send_y, back_recv_y, back_send_x, back_recv_x, back_send_z, back_recv_z,
-        f_all, f_recv_y, f_send_x, f_recv_x, f_send_z, f_recv_z,
+        back_send_o, back_recv_o, back_send_m, back_recv_m, back_send_x, back_recv_x, back_send_z, back_recv_z,
+        f_all, f_send_o, f_recv_o, f_send_m, f_recv_m, f_send_x, f_recv_x, f_send_z, f_recv_z,
         send_sems, recv_sems, arg_sems,
     ) = refs[28:]
     (
@@ -99,15 +100,23 @@
     unit = 8
     blocks = atoms // sends + 27
 
-    def step(axis, by):
-        size = lax.axis_size(axis)
-        return {axis: lax.rem(lax.axis_index(axis) + size + by, size)}
+    parity = lax.rem(lax.axis_index("gy"), 2)
+    plane_by = {OTHER: 2 * parity - 1, OWN: 0, MATE: 1 - 2 * parity}
+
+    def device(plane=OWN, **steps):
+        result = {}
+        if plane != OWN:
+            steps["gy"] = plane_by[plane]
+        for axis, by in steps.items():
+            size = lax.axis_size(axis)
+            result[axis] = lax.rem(lax.axis_index(axis) + size + by, size)
+        return result
 
     barrier = pltpu.get_barrier_semaphore()
-    for axis in ("gx", "gy", "gz"):
-        for by in (1, -1):
-            pl.semaphore_signal(barrier, inc=1, device_id=step(axis, by), device_id_type=MESH)
-
+    greeted = [device(gz=by) for by in (1, -1)] + [device(gx=by) for by in (1, -1)]
+    greeted += [device(OTHER), device(MATE)] + [device(OTHER, gx=by) for by in (1, -1)]
+    for other in greeted:
+        pl.semaphore_signal(barrier, inc=1, device_id=other, device_id_type=MESH)
     loads = [
         pltpu.make_async_copy(source, target, arg_sems.at[i])
         for i, (source, target) in enumerate(zip(args, held))
@@ -118,44 +127,59 @@
     next_sem = [0]
     started = []
 
-    def send(source, target, axis, by):
+    def send(source, target, other):
         slot = next_sem[0]
         next_sem[0] = slot + 1
         copy = pltpu.make_async_remote_copy(
             src_ref=source, dst_ref=target, send_sem=send_sems.at[slot], recv_sem=recv_sems.at[slot],
-            device_id=step(axis, by), device_id_type=MESH,
+            device_id=other, device_id_type=MESH,
         )
         copy.start()
         started.append(copy)
         return copy
 
-    def spread(ref, size, between):
-        def at(b, a, c):
-            return ref.at[pl.ds(position(b, a, c) * size, size)]
-
-        def along(axis, b, a, c):
-            sides = {"gz": ((b, a, 0), (b, a, 2)), "gx": ((b, 0, c), (b, 2, c)), "gy": ((0, a, c), (2, a, c))}
-            return [send(at(b, a, c), at(*side), axis, by) for side, by in zip(sides[axis], (1, -1))]
+    def settle(count):
+        for copy in started[:count]:
+            copy.wait_send()
+        del started[:count]
+
+    def spread(ref, size, pieces, between):
+        def at(b, a, c, piece):
+            return ref.at[pl.ds(position(b, a, c) * size + piece * (size // pieces), size // pieces)]
 
         def arrived(copies):
             for copy in copies:
                 copy.wait_recv()
 
-        in_z = along("gz", 1, 1, 1)
-        in_x = along("gx", 1, 1, 1)
-        in_y = along("gy", 1, 1, 1)
+        def along(c, piece):
+            return [send(at(OWN, 1, c, piece), at(OWN, a, c, piece), device(gx=1 - a)) for a in (0, 2)]
+
+        def across(a, c, piece):
+            return [send(at(OWN, a, c, piece), at(b, a, c, piece), device(b)) for b in (OTHER, MATE)]
+
+        every = range(pieces)
+        in_z = [
+            [send(at(OWN, 1, 1, piece), at(OWN, 1, c, piece), device(gz=1 - c)) for c in (0, 2)] for piece in every
+        ]
+        in_x = [along(1, piece) for piece in every]
+        near, last = [], []
+        for piece in every:
+            near += across(1, 1, piece)
         between[0]()
-        arrived(in_x)
-        in_y += along("gy", 1, 0, 1) + along("gy", 1, 2, 1)
-        arrived(in_z)
-        in_x = along("gx", 1, 1, 0) + along("gx", 1, 1, 2)
-        in_y += along("gy", 1, 1, 0) + along("gy", 1, 1, 2)
+        for piece in every:
+            arrived(in_x[piece])
+            near += across(0, 1, piece) + across(2, 1, piece)
+        in_x = []
+        for piece in every:
+            arrived(in_z[piece])
+            in_x.append(along(0, piece) + along(2, piece))
+            near += across(1, 0, piece) + across(1, 2, piece)
         between[1]()
-        arrived(in_x)
-        last = []
-        for c in (0, 2):
-            last += along("gy", 1, 0, c) + along("gy", 1, 2, c)
-        arrived(in_y)
+        for piece in every:
+            arrived(in_x[piece])
+            for c in (0, 2):
+                last += across(0, c, piece) + across(2, c, piece)
+        arrived(near)
         between[2]()
         arrived(last)
 
@@ -169,8 +193,8 @@
     lend_wide = mm_nt(eye(128, sends), lend_t).astype(BF16)
     lend = lend_wide[:sends]
     species_rows = jnp.broadcast_to(species[...].astype(F32), (unit, atoms))
-    kinds[pl.ds(position(1, 1, 1) * unit, unit), :] = mm_nt(species_rows.astype(BF16), lend_wide)
-    pl.semaphore_wait(barrier, 6)
+    kinds[pl.ds(position(OWN, 1, 1) * unit, unit), :] = mm_nt(species_rows.astype(BF16), lend_wide)
+    pl.semaphore_wait(barrier, len(greeted))
 
 
     def geometry():
@@ -207,7 +231,10 @@
         middle = jnp.where(live, center[...], -1)
         block = lax.shift_right_arithmetic(place, sends.bit_length() - 1)
         slot = lax.bitwise_and(place, sends - 1)
-        order = {position(b, a, c): (a * 3 + b) * 3 + c for a in range(3) for b in range(3) for c in range(3)}
+        planes = {plane: 1 + by for plane, by in plane_by.items()}
+        order = {
+            position(b, a, c): (a * 3 + planes[b]) * 3 + c for a in range(3) for b in planes for c in range(3)
+        }
         rows = lax.broadcasted_iota(jnp.int32, (32, 1), 0)
         block_ids = rows
         for i in range(27):
@@ -274,7 +301,7 @@
 
     root = math.sqrt(3.0)
     hid = w_rad0.shape[2]
-    spread(kinds, unit, (geometry, radial, lambda: None))
+    spread(kinds, unit, 1, (geometry, radial, lambda: None))
     number = species_rows[:1]
     kind_rows = [number] + [pltpu.roll(number, atoms - j * sends, 1) for j in range(1, atoms // sends)]
     kind_rows += [kinds[pl.ds(i * unit, 1), :] for i in range(27)]
@@ -305,9 +332,9 @@
     tensors = (gathered_t * gates).astype(BF16)
     proj2 = mm(w_src[1], scalars).astype(BF16)
     local = jnp.concatenate([proj2[:width], tensors], axis=0)
-    halo[pl.ds(position(1, 1, 1) * sends, sends), :] = mm_nt(lend, local).astype(BF16)
+    halo[pl.ds(position(OWN, 1, 1) * sends, sends), :] = mm_nt(lend, local).astype(BF16)
     table[:, pl.ds(0, atoms)] = local
-    nothing = lambda: None
+    earlier = len(started)
 
     def lookup(span):
         picked[:, span] = mm(table[...], onehot[pl.ds(0, early), span]).astype(BF16)
@@ -316,7 +343,7 @@
         table[:, pl.ds(atoms, early - atoms)] = halo[pl.ds(0, early - atoms), :].T
         sweep(edges, lookup)
 
-    spread(halo, sends, (nothing, nothing, early_rows))
+    spread(halo, sends, 1, (lambda: settle(earlier), lambda: None, early_rows))
     last_table[...] = halo[pl.ds(early - atoms, 2 * corner), :].T
 
     def layer_two(span):
@@ -349,16 +376,50 @@
             dmsg[pl.ds(width + m * chan, chan), span] = (d_inv * harm[pl.ds(m, 1), span]).astype(BF16)
 
     sweep(edges, back_two)
-    back_y = {}
-    parity = lax.rem(lax.axis_index("gy"), 2)
-    for slot, by in ((0, 2 * parity - 1), (1, 1 - 2 * parity)):
-        side = (by + 1) // 2
-        for piece, first, size, count in ((1, 9 * sends + 2 * rest, corner, corner), (0, 9 * sends, rest, rest)):
-            rows = pl.ds(rest if piece else 0, size)
-            start_row = pl.multiple_of(atoms + first + side * count, sends)
-            back_send_y[slot, rows] = mm_nt(onehot[pl.ds(start_row, size), :], dmsg[...]).astype(BF16)
-            back_y[slot, piece] = send(back_send_y.at[slot, rows], back_recv_y.at[slot, rows], "gy", by)
-    back = mm_nt(onehot[pl.ds(atoms, rows_y), :], dmsg[...])
+    earlier = len(started)
+
+    def scattered(plane, corners):
+        first = atoms + position(plane, *PLANE[REST if corners else 0][::-1]) * sends
+        return mm_nt(onehot[pl.ds(first, corner if corners else rest), :], dmsg[...])
+
+    def rows_of(c, a):
+        return pl.ds(PLANE.index((c, a)) * sends, sends)
+
+    halves = {True: pl.ds(rest, corner), False: pl.ds(0, rest)}
+    back_o, back_m, back_x, plane = {}, {}, {}, {}
+
+    def over(c, a):
+        rows = rows_of(c, a)
+        back_o[c, a] = send(back_send_o.at[rows], back_recv_o.at[rows], device(OTHER, gx=a - 1))
+
+    def to_mate(corners):
+        rows = halves[corners]
+        back_send_m[rows] = scattered(MATE, corners).astype(BF16)
+        back_m[corners] = send(back_send_m.at[rows], back_recv_m.at[rows], device(MATE))
+
+    def own_rows(corners):
+        sums = scattered(OWN, corners)
+        back_m[corners].wait_recv()
+        sums = sums + back_recv_m[halves[corners]].astype(F32)
+        cells = PLANE[REST:] if corners else PLANE[:REST]
+        for i, cell in enumerate(cells):
+            plane[cell] = sums[i * sends : (i + 1) * sends]
+        for c, a in cells:
+            if a != 1:
+                rows = rows_of(c, a)
+                back_send_x[rows] = plane[c, a].astype(BF16)
+                back_x[c, a] = send(back_send_x.at[rows], back_recv_x.at[rows], device(gx=a - 1))
+
+    back_send_o[halves[True]] = scattered(OTHER, True).astype(BF16)
+    for cell in PLANE[REST:]:
+        over(*cell)
+    to_mate(True)
+    own_rows(True)
+    back_send_o[halves[False]] = scattered(OTHER, False).astype(BF16)
+    for cell in PLANE[:REST]:
+        over(*cell)
+    to_mate(False)
+    own_rows(False)
     d_local = mm_nt(dmsg[...], onehot[pl.ds(0, atoms), :])
 
     def edge_two(span):
@@ -375,38 +436,24 @@
 
     sweep(edges, edge_two)
 
-    def merged(piece):
-        rows = pl.ds(rest if piece else 0, corner if piece else rest)
-        for slot in range(2):
-            back_y[slot, piece].wait_recv()
-        return (
-            back[rows.start : rows.start + rows.size]
-            + back_recv_y[0, rows].astype(F32) + back_recv_y[1, rows].astype(F32)
-        )
-
-    back_x = {}
-    plane = {}
-    for piece in (1, 0):
-        sums = merged(piece)
-        for i, (c, a) in enumerate(PLANE[REST:] if piece else PLANE[:REST]):
-            plane[c, a] = sums[i * sends : (i + 1) * sends]
-        for c in (0, 2) if piece else (1,):
-            for slot, part, by in ((0, 0, -1), (1, 2, 1)):
-                rows = pl.ds(c * sends, sends)
-                back_send_x[slot, rows] = plane[c, part].astype(BF16)
-                back_x[slot, c] = send(back_send_x.at[slot, rows], back_recv_x.at[slot, rows], "gx", by)
-
-    def gathered_x(c):
-        rows = pl.ds(c * sends, sends)
-        for slot in range(2):
-            back_x[slot, c].wait_recv()
-        return plane[c, 1] + back_recv_x[0, rows].astype(F32) + back_recv_x[1, rows].astype(F32)
+    settle(earlier)
+
+    def gathered(c):
+        total = plane[c, 1]
+        for a in range(3):
+            back_o[c, a].wait_recv()
+            total = total + back_recv_o[rows_of(c, a)].astype(F32)
+        for a in (0, 2):
+            back_x[c, a].wait_recv()
+            total = total + back_recv_x[rows_of(c, a)].astype(F32)
+        return total
 
     back_z = []
-    for slot, part, by in ((0, 0, -1), (1, 2, 1)):
-        back_send_z[slot] = gathered_x(part).astype(BF16)
-        back_z.append(send(back_send_z.at[slot], back_recv_z.at[slot], "gz", by))
-    back = gathered_x(1)
+    for slot, c in ((0, 0), (1, 2)):
+        back_send_z[slot] = gathered(c).astype(BF16)
+        back_z.append(send(back_send_z.at[slot], back_recv_z.at[slot], device(gz=c - 1)))
+    back = gathered(1)
+    settle(len(started) - 2)
     for copy in back_z:
         copy.wait_recv()
     back = back + back_recv_z[0].astype(F32) + back_recv_z[1].astype(F32)
@@ -458,41 +505,41 @@
         ).astype(BF16)
     f_all[...] = mm_nt(f_rows[...], slot_of[...])
     first = (atoms // sends) * unit
-    f_y = []
-    for slot, part, by in ((0, 0, -1), (1, 2, 1)):
-        for index, count in ((REST, 9 - REST), (0, REST)):
-            c, a = PLANE[index]
-            f_y.append(send(
-                f_all.at[pl.ds(first + position(part, a, c) * unit, count * unit)],
-                f_recv_y.at[slot, pl.ds(index * unit, count * unit)], "gy", by,
-            ))
+
+    def cell(b, a, c):
+        return f_all[pl.ds(first + position(b, a, c) * unit, unit), :]
+
+    for a in range(3):
+        f_send_o[a] = jnp.concatenate([cell(OTHER, a, c) for c in range(3)], axis=0)
+    f_send_m[...] = jnp.concatenate([cell(MATE, a, c) for a in range(3) for c in range(3)], axis=0)
+    f_m = send(f_send_m, f_recv_m, device(MATE))
+    f_o = [send(f_send_o.at[a], f_recv_o.at[a], device(OTHER, gx=a - 1)) for a in (0, 2, 1)]
+    lines = jnp.concatenate([cell(OWN, a, c) for a in range(3) for c in range(3)], axis=0)
+    f_m.wait_recv()
+    lines = lines + f_recv_m[...]
+    f_x = []
+    for slot, a in ((0, 0), (1, 2)):
+        f_send_x[slot] = lines[3 * a * unit : 3 * (a + 1) * unit]
+        f_x.append(send(f_send_x.at[slot], f_recv_x.at[slot], device(gx=a - 1)))
     total = mm_nt(pulls.astype(BF16), onehot_c[...])
     for j in range(atoms // sends):
         block = f_all[pl.ds(j * unit, unit), :]
         total = total - (block if j == 0 else pltpu.roll(block, j * sends, 1))
-    for copy in f_y:
+    settle(len(started) - 2)
+    for copy in f_x + f_o:
         copy.wait_recv()
-    lines = f_all[pl.ds(first, 9 * unit), :] + f_recv_y[0] + f_recv_y[1]
-    cells = {cell: lines[i * unit : (i + 1) * unit] for i, cell in enumerate(PLANE)}
-    f_x = []
-    for slot, part, by in ((0, 0, -1), (1, 2, 1)):
-        f_send_x[slot] = jnp.concatenate([cells[c, part] for c in range(3)], axis=0)
-        f_x.append(send(f_send_x.at[slot], f_recv_x.at[slot], "gx", by))
-    for copy in f_x:
-        copy.wait_recv()
-    lines = jnp.concatenate([cells[c, 1] for c in range(3)], axis=0) + f_recv_x[0] + f_recv_x[1]
+    lines = lines[3 * unit : 6 * unit] + f_recv_x[0] + f_recv_x[1] + f_recv_o[0] + f_recv_o[1] + f_recv_o[2]
     f_z = []
-    for slot, part, by in ((0, 0, -1), (1, 2, 1)):
-        f_send_z[slot] = lines[part * unit : (part + 1) * unit]
-        f_z.append(send(f_send_z.at[slot], f_recv_z.at[slot], "gz", by))
+    for slot, c in ((0, 0), (1, 2)):
+        f_send_z[slot] = lines[c * unit : (c + 1) * unit]
+        f_z.append(send(f_send_z.at[slot], f_recv_z.at[slot], device(gz=c - 1)))
     for copy in f_z:
         copy.wait_recv()
     lines = lines[unit : 2 * unit] + f_recv_z[0] + f_recv_z[1]
     total = total - joined(mm(split(lines), lend_wide))
     for row in range(3):
         forces[row] = total[row : row + 1] + total[row + 3 : row + 4]
-    for copy in started:
-        copy.wait_send()
+    settle(len(started))
 
 
 def per_device(
@@ -512,7 +559,7 @@
     vmem = pl.BlockSpec(memory_space=pltpu.VMEM)
     smem = pl.BlockSpec(memory_space=pltpu.SMEM)
     hbm = pl.BlockSpec(memory_space=pltpu.HBM)
-    copies = 26 + 26 + 12 + 8
+    copies = 26 + 26 * 1 + 19 + 8
     operands = (
         species.reshape(1, atoms), send_list.reshape(1, sends), edge_vectors.reshape(3, 1, edges),
         edge_neighbour.reshape(1, edges), edge_center.reshape(1, edges),
@@ -559,14 +606,19 @@
             pltpu.VMEM((8, edges), F32),
             pltpu.VMEM((1, edges), F32),
             pltpu.VMEM((8, edges), F32),
-            pltpu.VMEM((2, 9 * sends, cols), BF16),
-            pltpu.VMEM((2, 9 * sends, cols), BF16),
-            pltpu.VMEM((2, 3 * sends, cols), BF16),
-            pltpu.VMEM((2, 3 * sends, cols), BF16),
+            pltpu.VMEM((9 * sends, cols), BF16),
+            pltpu.VMEM((9 * sends, cols), BF16),
+            pltpu.VMEM((9 * sends, cols), BF16),
+            pltpu.VMEM((9 * sends, cols), BF16),
+            pltpu.VMEM((9 * sends, cols), BF16),
+            pltpu.VMEM((9 * sends, cols), BF16),
             pltpu.VMEM((2, sends, cols), BF16),
             pltpu.VMEM((2, sends, cols), BF16),
             pltpu.VMEM((32 * unit, 128), F32),
-            pltpu.VMEM((2, 9 * unit, 128), F32),
+            pltpu.VMEM((3, 3 * unit, 128), F32),
+            pltpu.VMEM((3, 3 * unit, 128), F32),
+            pltpu.VMEM((9 * unit, 128), F32),
+            pltpu.VMEM((9 * unit, 128), F32),
             pltpu.VMEM((2, 3 * unit, 128), F32),
             pltpu.VMEM((2, 3 * unit, 128), F32),
             pltpu.VMEM((2, unit, 128), F32),

time: 70.7 us -> 69.7 us (0.986)
  no operation moved by 1% of the time
where the time goes in v3:
time: 69.7 us; the launch traced here: 69.5 us
  Pallas kernels  65.9 us (95%)
  between operations  1.95 us (3%)
  local copies, waits for them, and re-layouts  1.69 us (2%)
    pallas_call x1, Pallas kernels, per_device(): pl.pallas_call(body, out_shape=(jax.ShapeDtypeStruct((1, atoms), F32), ja...  65.9 us
    unnamed x6, local copies, waits for them, and re-layouts  1.69 us

profile of v3, /device:TPU:1, one launch (start us, length us, event | category | flops | bytes accessed | tf_op | source)
XLA Modules:
  0.0 69.5 jit_solution(13375333171191435497)
XLA Ops:
  1.9 65.9 %shard_map.158 = (f32[1,128]{1,0:T(1,128)}, f32[3,1,128]{2,1,0:T(1,128)}) custom-call(s32[1,1,1]{2,1,0:T(1,128)S(6)} %copy.20.atom_count, s32[1,1,1]{2,1,0:T(1,128)S(6)} %copy.21.edge_count, s32[1,128]{1,0:T(1,128)} %bitcast.18, s32[1,32]{1,0:T(1,128)} %bitcast.19, f32[3,1,2560]{2,1,0:T(1,128)} %bitcast.14, s32[1,2560]{1,0:T(1,128)} %bitcast.15, ...), custom_call_target="tpu_custom_call" | custom-call | tf_op jit(solution)/shard_map/pallas_call | solution.py:569
  67.8 0.0 copy-start.1
  67.8 0.0 copy-start
  67.8 0.6 copy-done.1
  68.4 0.5 copy.22
  69.0 0.0 copy-done
  69.0 0.6 copy.23
Async XLA Ops:
  67.8 0.6 copy-start.1
  67.8 1.1 %copy-start = (f32[3,1,128]{2,1,0:T(1,128)S(1)}, f32[3,1,128]{2,1,0:T(1,128)}, u32[]{:S(2)}) copy-start(f32[3,1,128]{2,1,0:T(1,128)} %get-tuple-element.5) | copy-start | bytes 4612

commit v4 on v3

--- a/solution.py
+++ b/solution.py
@@ -112,16 +112,19 @@
             result[axis] = lax.rem(lax.axis_index(axis) + size + by, size)
         return result
 
+    loads = [
+        pltpu.make_async_copy(source, target, arg_sems.at[i])
+        for i, (source, target) in enumerate(zip(args, held))
+    ]
+    for load in loads[:2]:
+        load.start()
+
     barrier = pltpu.get_barrier_semaphore()
     greeted = [device(gz=by) for by in (1, -1)] + [device(gx=by) for by in (1, -1)]
     greeted += [device(OTHER), device(MATE)] + [device(OTHER, gx=by) for by in (1, -1)]
     for other in greeted:
         pl.semaphore_signal(barrier, inc=1, device_id=other, device_id_type=MESH)
-    loads = [
-        pltpu.make_async_copy(source, target, arg_sems.at[i])
-        for i, (source, target) in enumerate(zip(args, held))
-    ]
-    for load in loads:
+    for load in loads[2:5]:
         load.start()
 
     next_sem = [0]
@@ -143,7 +146,9 @@
             copy.wait_send()
         del started[:count]
 
-    def spread(ref, size, pieces, between):
+    def spread(ref, size, pieces, between, straight=False):
+        near, last = [], []
+
         def at(b, a, c, piece):
             return ref.at[pl.ds(position(b, a, c) * size + piece * (size // pieces), size // pieces)]
 
@@ -152,17 +157,20 @@
                 copy.wait_recv()
 
         def along(c, piece):
-            return [send(at(OWN, 1, c, piece), at(OWN, a, c, piece), device(gx=1 - a)) for a in (0, 2)]
+            copies = [send(at(OWN, 1, c, piece), at(OWN, a, c, piece), device(gx=1 - a)) for a in (0, 2)]
+            for a in (0, 2) if straight else ():
+                last.append(send(at(OWN, 1, c, piece), at(OTHER, a, c, piece), device(OTHER, gx=1 - a)))
+            return copies
 
         def across(a, c, piece):
-            return [send(at(OWN, a, c, piece), at(b, a, c, piece), device(b)) for b in (OTHER, MATE)]
+            planes = (MATE,) if straight and a != 1 else (OTHER, MATE)
+            return [send(at(OWN, a, c, piece), at(b, a, c, piece), device(b)) for b in planes]
 
         every = range(pieces)
         in_z = [
             [send(at(OWN, 1, 1, piece), at(OWN, 1, c, piece), device(gz=1 - c)) for c in (0, 2)] for piece in every
         ]
         in_x = [along(1, piece) for piece in every]
-        near, last = [], []
         for piece in every:
             near += across(1, 1, piece)
         between[0]()
@@ -198,6 +206,8 @@
 
 
     def geometry():
+        for load in loads[5:]:
+            load.start()
         for load in loads[2:5]:
             load.wait()
         live = lax.broadcasted_iota(jnp.int32, (1, edges), 1) < edge_count[0, 0, 0]
@@ -301,7 +311,7 @@
 
     root = math.sqrt(3.0)
     hid = w_rad0.shape[2]
-    spread(kinds, unit, 1, (geometry, radial, lambda: None))
+    spread(kinds, unit, 1, (geometry, radial, lambda: None), straight=True)
     number = species_rows[:1]
     kind_rows = [number] + [pltpu.roll(number, atoms - j * sends, 1) for j in range(1, atoms // sends)]
     kind_rows += [kinds[pl.ds(i * unit, 1), :] for i in range(27)]

time: 69.7 us -> 68.6 us (0.984)
  Pallas kernels: 65.9 us -> 64.8 us
    pallas_call x1, Pallas kernels: 65.9 us -> 64.8 us  [per_device(): pl.pallas_call(body, out_shape=(jax.ShapeDtypeStruct((1, atoms), F32), ja...]
where the time goes in v4:
time: 68.6 us; the launch traced here: 68.4 us
  Pallas kernels  64.8 us (94%)
  between operations  1.95 us (3%)
  local copies, waits for them, and re-layouts  1.69 us (2%)
    pallas_call x1, Pallas kernels, per_device(): pl.pallas_call(body, out_shape=(jax.ShapeDtypeStruct((1, atoms), F32), ja...  64.8 us
    unnamed x6, local copies, waits for them, and re-layouts  1.69 us

profile of v4, /device:TPU:1, one launch (start us, length us, event | category | flops | bytes accessed | tf_op | source)
XLA Modules:
  0.0 68.4 jit_solution(8779706950973632708)
XLA Ops:
  1.9 64.8 %shard_map.158 = (f32[1,128]{1,0:T(1,128)}, f32[3,1,128]{2,1,0:T(1,128)}) custom-call(s32[1,1,1]{2,1,0:T(1,128)S(6)} %copy.20.atom_count, s32[1,1,1]{2,1,0:T(1,128)S(6)} %copy.21.edge_count, s32[1,128]{1,0:T(1,128)} %bitcast.18, s32[1,32]{1,0:T(1,128)} %bitcast.19, f32[3,1,2560]{2,1,0:T(1,128)} %bitcast.14, s32[1,2560]{1,0:T(1,128)} %bitcast.15, ...), custom_call_target="tpu_custom_call" | custom-call | tf_op jit(solution)/shard_map/pallas_call | solution.py:579
  66.7 0.0 copy-start.1
  66.7 0.0 copy-start
  66.7 0.6 copy-done.1
  67.3 0.5 copy.22
  67.8 0.0 copy-done
  67.8 0.6 copy.23
Async XLA Ops:
  66.7 0.6 copy-start.1
  66.7 1.1 %copy-start = (f32[3,1,128]{2,1,0:T(1,128)S(1)}, f32[3,1,128]{2,1,0:T(1,128)}, u32[]{:S(2)}) copy-start(f32[3,1,128]{2,1,0:T(1,128)} %get-tuple-element.5) | copy-start | bytes 4612

commit v5 on v4

--- a/solution.py
+++ b/solution.py
@@ -198,10 +198,10 @@
     lend_t = jnp.where(
         lax.broadcasted_iota(jnp.int32, (atoms, sends), 0) == send_list[...], 1.0, 0.0
     ).astype(BF16)
-    lend_wide = mm_nt(eye(128, sends), lend_t).astype(BF16)
-    lend = lend_wide[:sends]
     species_rows = jnp.broadcast_to(species[...].astype(F32), (unit, atoms))
-    kinds[pl.ds(position(OWN, 1, 1) * unit, unit), :] = mm_nt(species_rows.astype(BF16), lend_wide)
+    own_kinds = pl.ds(position(OWN, 1, 1) * unit, unit)
+    kinds[own_kinds, :] = jnp.zeros((unit, atoms), F32)
+    kinds[own_kinds, pl.ds(0, sends)] = mm(species_rows.astype(BF16), lend_t)
     pl.semaphore_wait(barrier, len(greeted))
 
 
@@ -312,6 +312,9 @@
     root = math.sqrt(3.0)
     hid = w_rad0.shape[2]
     spread(kinds, unit, 1, (geometry, radial, lambda: None), straight=True)
+    lend_wide = mm_nt(eye(128, sends), lend_t).astype(BF16)
+    lend = lend_wide[:sends]
+
     number = species_rows[:1]
     kind_rows = [number] + [pltpu.roll(number, atoms - j * sends, 1) for j in range(1, atoms // sends)]
     kind_rows += [kinds[pl.ds(i * unit, 1), :] for i in range(27)]

time: 68.6 us -> 68.3 us (level)
  no operation moved by 1% of the time
where the time goes in v5:
time: 68.3 us; the launch traced here: 68.2 us
  Pallas kernels  64.5 us (94%)
  between operations  1.95 us (3%)
  local copies, waits for them, and re-layouts  1.69 us (2%)
    pallas_call x1, Pallas kernels, per_device(): pl.pallas_call(body, out_shape=(jax.ShapeDtypeStruct((1, atoms), F32), ja...  64.5 us
    unnamed x6, local copies, waits for them, and re-layouts  1.69 us

profile of v5, /device:TPU:1, one launch (start us, length us, event | category | flops | bytes accessed | tf_op | source)
XLA Modules:
  0.0 68.2 jit_solution(16606218521143014788)
XLA Ops:
  1.9 64.5 %shard_map.158 = (f32[1,128]{1,0:T(1,128)}, f32[3,1,128]{2,1,0:T(1,128)}) custom-call(s32[1,1,1]{2,1,0:T(1,128)S(6)} %copy.20.atom_count, s32[1,1,1]{2,1,0:T(1,128)S(6)} %copy.21.edge_count, s32[1,128]{1,0:T(1,128)} %bitcast.18, s32[1,32]{1,0:T(1,128)} %bitcast.19, f32[3,1,2560]{2,1,0:T(1,128)} %bitcast.14, s32[1,2560]{1,0:T(1,128)} %bitcast.15, ...), custom_call_target="tpu_custom_call" | custom-call | tf_op jit(solution)/shard_map/pallas_call | solution.py:582
  66.4 0.0 copy-start.1
  66.5 0.0 copy-start
  66.5 0.6 copy-done.1
  67.1 0.5 copy.22
  67.6 0.0 copy-done
  67.6 0.6 copy.23
Async XLA Ops:
  66.4 0.6 copy-start.1
  66.5 1.1 %copy-start = (f32[3,1,128]{2,1,0:T(1,128)S(1)}, f32[3,1,128]{2,1,0:T(1,128)}, u32[]{:S(2)}) copy-start(f32[3,1,128]{2,1,0:T(1,128)} %get-tuple-element.5) | copy-start | bytes 4612
